TPU v7x, 32 devices: a whole 2x2x4 slice. The times are simulated.
32 devices in a mesh: xs: 8 (over z, y), ys: 4 (over x, core).
Axes of the slice: x: 2, y: 2, z: 4, core: 2. Of those that a mesh axis runs over, the one named last changes fastest.
Arguments:
- multipoles: bfloat16 [121, 4096], P(None, ('xs', 'ys')), may hold values from -6 to 6
- translation_ops: bfloat16 [316, 121, 121], replicated, may hold values from -0.046875 to 0.046875
- target_interaction_table: int32 [316, 4096], P(None, ('xs', 'ys')), may hold values from -1 to 1151, as said below
- evaluation: bfloat16 [4, 121, 65536], P(None, None, ('xs', 'ys')), may hold values from -0.5 to 0.5
- ion_data: bfloat16 [4, 65536], P(None, ('xs', 'ys')), may hold values from -1 to 1
- atom_owner: int32 [65536, 1], P(('xs', 'ys')), may hold values from 0 to 31, as said below
- atom_slot: int32 [65536], P(('xs', 'ys')), may hold values from 0 to 127
Outputs:
- local_exp: bfloat16 [121, 4096], P(None, ('xs', 'ys'))
- atom_far_field: float32 [4, 65536], P(None, ('xs', 'ys'))
- box_virial: float32 [9, 4096], P(None, ('xs', 'ys'))
Inputs may be any that keep to these rules, and one draw needn't show every extreme that they name: `target_interaction_table`: box slot s of a device is (bx * 4 + by) * 8 + bz; device (ix, iy) holds the periodic grid's boxes of x from ix * 4, y from iy * 4 and all z. Row k stands for the k-th offset (dx, dy, dz) of -3..3 in each coordinate, dx slowest, dz fastest, leaving out those with all three of magnitude 1 or less. An entry is -1, or (3 * (ex + 1) + (ey + 1)) * 128 + s naming the box at that offset from the target: slot s of the device ex steps along xs and ey steps along ys away, ex and ey in -1, 0, 1. It is -1 where the offset along some coordinate lies outside -2 - q .. 3 - q, q the parity of the target's coordinate there, and where the box at that offset holds no ions; most boxes hold ions. `atom_owner`: the device is ix * 4 + iy; an atom held by device (ix, iy) names that device itself or one of the eight devices ((ix + ex) mod 8, (iy + ey) mod 4) with ex, ey in -1, 0, 1; among the atoms of one device at most 32 name the same other device, and in every device's atoms some other device is named exactly 32 times.
All inputs are finite; a program needn't handle non-finite values.
Results may differ from a plain program's by a relative error of at most 0.0029.
Values may be sent and summed in bfloat16 or wider, within the bound.
No kernel may reach another device: no remote copies, remote signals or barrier semaphores. Data moves between devices by JAX's collectives and lax.ppermute only.
A program may use at most 64 MiB of HBM per device.

v0:
```python
import jax
import jax.numpy as jnp
from jax import lax
from jax.sharding import PartitionSpec as P


def extended_2(block, sides, width):
    for axis, dim in sides:
        count = lax.axis_size(axis)
        forward = [(i, i + 1) for i in range(count - 1)]
        forward.append((count - 1, 0))
        backward = [(target, source) for source, target in forward]
        low = lax.ppermute(
            lax.slice_in_dim(block, block.shape[dim] - width, None, axis=dim), axis, forward
        )
        high = lax.ppermute(lax.slice_in_dim(block, 0, width, axis=dim), axis, backward)
        block = jnp.concatenate([low, block, high], axis=dim)
    return block


def virial_of(ions, values):
    charge = ions[0].astype(jnp.float32)
    position = ions[1:4].astype(jnp.float32)
    combined = charge[None, None, :] * position[:, None, :] * values[None, 1:4, :]
    return combined.reshape(9, values.shape[1])


def box_sums(virial_terms, safe_slots, capacity):
    summed = jax.ops.segment_sum(virial_terms.T, safe_slots, num_segments=capacity + 1)
    return summed[:capacity].T


def scatter_cols(source_box_index, place, incoming_row_data, fill_value, dtype):
    start = jnp.full((source_box_index.shape[0], incoming_row_data + 1), fill_value, dtype)
    return start.at[:, place].set(source_box_index)[:, :incoming_row_data]


def as_grid(buffer):
    return buffer.reshape(buffer.shape[0], 3, 3, buffer.shape[1] // 9)


def from_grid(extended):
    picked = extended[:, 0::2, 0::2, :]
    return picked.reshape(picked.shape[0], 9 * picked.shape[3])


def shards(
    multipoles,
    translation_ops,
    target_interaction_table,
    evaluation,
    ion_data,
    atom_owner,
    atom_slot,
):
    num_terms, capacity = multipoles.shape
    size_x = lax.axis_size("xs")
    size_y = lax.axis_size("ys")
    atoms_dev = atom_slot.shape[0]
    per_peer = atoms_dev // 64
    incoming_row_data = 9 * per_peer
    extended = extended_2(multipoles.reshape(num_terms, 1, 1, capacity), (("xs", 1), ("ys", 2)), 1)
    columns = jnp.concatenate(
        [extended.reshape(num_terms, 9 * capacity), jnp.zeros((num_terms, 1), jnp.bfloat16)], axis=1
    )
    entries = target_interaction_table
    entries = jnp.where(entries < 0, 9 * capacity, entries)
    gathered = jnp.take(columns, entries, axis=1)
    pieces = jnp.einsum(
        "kqp,pkt->qt", translation_ops, gathered, preferred_element_type=jnp.float32
    )
    local_exp = pieces.astype(jnp.bfloat16)
    padded_local = jnp.concatenate([local_exp, jnp.zeros((num_terms, 1), jnp.bfloat16)], axis=1)
    owners = atom_owner[:, 0]
    myself = lax.axis_index(("xs", "ys"))
    mine_x = myself // size_y
    mine_y = myself % size_y
    step_x = (owners // size_y - mine_x + 1) % size_x - 1
    stride_along_y = (owners % size_y - mine_y + 1) % size_y - 1
    offset = 3 * (step_x + 1) + stride_along_y + 1
    remote = owners != myself
    member = (
        (offset[:, None] == jnp.arange(9, dtype=jnp.int32)[None, :]) & remote[:, None]
    ).astype(jnp.int32)
    previous_level = jnp.cumsum(member, axis=0) - member
    place = jnp.where(
        remote, offset * per_peer + jnp.sum(previous_level * member, axis=1), incoming_row_data
    )
    local_slots = jnp.where(remote, capacity, atom_slot)
    own_cols = jnp.take(padded_local, atom_slot, axis=1)
    requests = scatter_cols(atom_slot[None, :], place, incoming_row_data, -1, jnp.int32)
    slots = from_grid(extended_2(as_grid(requests), (("xs", 1), ("ys", 2)), 1))[0]
    safe_slots = jnp.where(slots < 0, capacity, slots)
    box_cols = jnp.take(padded_local, safe_slots, axis=1)
    returned = from_grid(extended_2(as_grid(box_cols), (("xs", 1), ("ys", 2)), 1))
    returned = jnp.concatenate([returned, jnp.zeros((num_terms, 1), jnp.bfloat16)], axis=1)
    far_cols = jnp.take(returned, place, axis=1)
    atom_column_list = jnp.where(remote[None, :], far_cols, own_cols)
    atom_far_field = jnp.einsum(
        "zuq,uq->zq", evaluation, atom_column_list, preferred_element_type=jnp.float32
    )
    terms = virial_of(ion_data, atom_far_field)
    outgoing = scatter_cols(terms, place, incoming_row_data, 0.0, jnp.float32)
    incoming = from_grid(extended_2(as_grid(outgoing), (("xs", 1), ("ys", 2)), 1))
    box_virial = box_sums(incoming, safe_slots, capacity) + box_sums(terms, local_slots, capacity)
    return (local_exp, atom_far_field, box_virial)


def solution(mesh):
    placed = (
        P(None, ("xs", "ys")),
        P(),
        P(None, ("xs", "ys")),
        P(None, None, ("xs", "ys")),
        P(None, ("xs", "ys")),
        P(("xs", "ys"), None),
        P(("xs", "ys")),
    )
    return jax.shard_map(
        shards,
        mesh=mesh,
        in_specs=placed,
        out_specs=(P(None, ("xs", "ys")), P(None, ("xs", "ys")), P(None, ("xs", "ys"))),
        check_vma=False,
    )
```

profile of v0, /device:TPU:0, one launch (start us, length us, event | category | flops | bytes accessed | tf_op | source)
XLA Modules:
  0.0 194.7 jit_solution(4220065558543768160)
XLA Ops:
  0.6 6.1 %collective-permute-start.1 = (bf16[121,1,1,128]{3,0,2,1:T(8,128)(2,1)}, bf16[121,1,1,128]{3,0,2,1:T(8,128)(2,1)S(1)}, u32[]{:S(2)}, u32[]{:S(2)}) collective-permute-start(bf16[121,1,1,128]{3,0,2,1:T(8,128)(2,1)} %bitcast.73), channel_id=1, source_target_pairs={{4,0},{8,4},{12,8},{16,12},{20,16},{24,20},{28,24},{0,28},{5,1},{9... | collective-permute-start | bytes 92936 | tf_op jit(solution)/shard_map/ppermute | solution.py:16
  7.4 0.8 fusion.43
  8.3 2.6 %reduce-window.6 = s32[9,16,128]{2,1,0:T(8,128)S(1)} reduce-window(s32[9,16,128]{2,1,0:T(8,128)S(1)} %fusion.31, s32[]{:T(128)} %constant.127.clone.1), window={size=1x1x128 pad=0_0x0_0x127_0}, to_apply=%region_0.1 | reduce-window | flops 2340864 | bytes 147460 | tf_op jit(solution)/shard_map/reduce-window
  11.6 0.9 and_reduce_fusion
  12.5 8.2 %scatter_custom_fusion = s32[289]{0:T(512)S(1)} fusion(s32[2048]{0:T(1024)S(1)} %bitcast.83, s32[2048]{0:T(1024)} %param.13, s32[]{:T(128)} %constant.139.clone.1), kind=kCustom, calls=%fused_computation.98 | custom fusion | bytes 1668 | tf_op jit(solution)/shard_map/scatter | solution.py:35
  20.8 4.8 %collective-permute-start.5 = (s32[1,1,3,32]{3,2,1,0:T(4,128)S(1)}, s32[1,1,3,32]{3,2,1,0:T(4,128)S(1)}, u32[]{:S(2)}, u32[]{:S(2)}) collective-permute-start(s32[1,1,3,32]{3,2,1,0:T(4,128)S(1)} %get-tuple-element.28), channel_id=1, source_target_pairs={{4,0},{8,4},{12,8},{16,12},{20,16},{24,20},{28,24},{0,28},{5,1},{9... | collective-permute-start | bytes 1160 | tf_op jit(solution)/shard_map/ppermute | solution.py:16
  25.6 0.9 fusion.28
  27.3 0.7 convert_multiply_fusion
  28.6 1.0 compare_and_fusion
  29.6 1.6 collective-permute-done.6
  31.5 0.8 pad_maximum_fusion.3
  32.9 1.7 collective-permute-done.3
  34.6 2.9 %collective-permute-done.2 = bf16[121,3,1,128]{3,0,2,1:T(8,128)(2,1)S(1)} collective-permute-done((bf16[121,3,1,128]{3,0,2,1:T(8,128)(2,1)S(1)}, bf16[121,3,1,128]{3,0,2,1:T(8,128)(2,1)S(1)}, u32[]{:S(2)}, u32[]{:S(2)}) %collective-permute-start.2) | collective-permute-done | bytes 92960 | tf_op jit(solution)/shard_map/ppermute | solution.py:13
  37.5 0.8 pad_maximum_fusion
  38.6 81.1 %gather_fusion = bf16[40448,121]{1,0:T(8,128)(2,1)} fusion(bf16[121,1153]{0,1:T(8,128)(2,1)S(1)} %concatenate.35, s32[40960]{0:T(1024)S(1)} %pad_clamp_fusion), kind=kCustom, calls=%fused_computation | custom fusion | bytes 19738624 | tf_op jit(solution)/shard_map/jit(_take)/gather | solution.py:68
  119.6 16.7 %fusion.16 = bf16[121,128]{0,1:T(8,128)(2,1)S(1)} fusion(bf16[316,121,121]{2,0,1:T(8,128)(2,1)} %param.8, bf16[316,128,121]{2,1,0:T(8,128)(2,1)} %bitcast.63, pred[316,128]{1,0:T(8,128)(4,1)S(1)} %compare_and_fusion), kind=kOutput, calls=%fused_computation.17 | convolution fusion | flops 1189308032 | bytes 19112952 | tf_op jit(solution)/shard_map/kqp,pkt->qt/dot_general | solution.py:69
  136.4 1.4 gather_fusion.1
  137.9 3.7 %collective-permute-start.9 = (bf16[121,1,3,32]{0,3,2,1:T(8,128)(2,1)S(1)}, bf16[121,1,3,32]{0,3,2,1:T(8,128)(2,1)S(1)}, u32[]{:S(2)}, u32[]{:S(2)}) collective-permute-start(bf16[121,1,3,32]{0,3,2,1:T(8,128)(2,1)S(1)} %get-tuple-element.21), channel_id=1, source_target_pairs={{4,0},{8,4},{12,8},{16,12},{20,16},{24,20},{28,24},{0,28},{5,1},{9... | collective-permute-start | bytes 69704 | tf_op jit(solution)/shard_map/ppermute | solution.py:16
  141.6 1.5 collective-permute-done.9
  143.1 5.0 %collective-permute-done.8 = bf16[121,1,3,32]{0,3,2,1:T(8,128)(2,1)S(1)} collective-permute-done((bf16[121,1,3,32]{0,3,2,1:T(8,128)(2,1)S(1)}, bf16[121,1,3,32]{0,3,2,1:T(8,128)(2,1)S(1)}, u32[]{:S(2)}, u32[]{:S(2)}) %collective-permute-start.8) | collective-permute-done | bytes 23264 | tf_op jit(solution)/shard_map/ppermute | solution.py:13
  148.7 6.2 %gather_fusion.3 = bf16[2048,121]{1,0:T(8,128)(2,1)S(1)} fusion(bf16[121,129]{0,1:T(8,128)(2,1)S(1)} %concatenate.38, s32[2048]{0:T(1024)S(1)} %get-tuple-element.27), kind=kCustom, calls=%fused_computation.3 | custom fusion | bytes 999424 | tf_op jit(solution)/shard_map/jit(_take)/gather | solution.py:90
  155.0 6.2 %gather_fusion.2 = bf16[2048,121]{1,0:T(8,128)(2,1)S(1)} fusion(bf16[121,289]{0,1:T(8,128)(2,1)S(1)} %concatenate.41, s32[2048]{0:T(1024)S(1)} %get-tuple-element.30), kind=kCustom, calls=%fused_computation.2 | custom fusion | bytes 999424 | tf_op jit(solution)/shard_map/jit(_take)/gather | solution.py:97
  161.2 1.0 select_convert_fusion
  162.6 2.7 %multiply_reduce_fusion = f32[2048,4]{0,1:T(4,128)S(1)} fusion(f32[2048,121]{0,1:T(8,128)S(1)} %copy.38, bf16[4,121,2048]{2,0,1:T(4,128)(2,1)} %param.10), kind=kLoop, calls=%fused_computation.14 | loop fusion | flops 2965504 | bytes 3006464 | tf_op jit(solution)/shard_map/zuq,uq->zq/dot_general | solution.py:99
  165.7 5.7 %scatter_custom_fusion.1 = f32[9,289]{0,1:T(8,128)S(1)} fusion(s32[2048]{0:T(1024)S(1)} %bitcast.85, f32[9,2048]{0,1:T(8,128)S(1)} %copy.23, f32[]{:T(128)} %constant.147.clone.1), kind=kCustom, calls=%fused_computation.20 | custom fusion | bytes 1058984 | tf_op jit(solution)/shard_map/scatter | solution.py:35
  171.7 2.0 %collective-permute-start.12 = (f32[9,1,3,32]{3,2,1,0:T(4,128)S(1)}, f32[9,1,3,32]{3,2,1,0:T(4,128)S(1)}, u32[]{:S(2)}, u32[]{:S(2)}) collective-permute-start(f32[9,1,3,32]{3,2,1,0:T(4,128)S(1)} %get-tuple-element.22), channel_id=1, source_target_pairs={{0,4},{4,8},{8,12},{12,16},{16,20},{20,24},{24,28},{28,0},{1,5},{5... | collective-permute-start | bytes 10376 | tf_op jit(solution)/shard_map/ppermute | solution.py:13
  173.7 1.7 collective-permute-done.13
  175.4 2.8 %collective-permute-done.12 = f32[9,1,3,32]{3,2,1,0:T(4,128)S(1)} collective-permute-done((f32[9,1,3,32]{3,2,1,0:T(4,128)S(1)}, f32[9,1,3,32]{3,2,1,0:T(4,128)S(1)}, u32[]{:S(2)}, u32[]{:S(2)}) %collective-permute-start.12) | collective-permute-done | bytes 3488 | tf_op jit(solution)/shard_map/ppermute | solution.py:13
  178.8 0.7 copy.28
  179.6 11.5 %scatter_custom_fusion.3 = f32[129,9]{1,0:T(8,128)S(1)} fusion(s32[2048]{0:T(1024)S(1)} %get-tuple-element.26, f32[9,2048]{0,1:T(8,128)S(1)} %copy.23, f32[]{:T(128)} %constant.147.clone.1), kind=kCustom, calls=%fused_computation.18 | custom fusion | flops 18432 | bytes 1053224 | tf_op jit(solution)/shard_map/scatter-add | solution.py:29
  191.2 1.0 slice.93
  192.3 1.8 scatter_custom_fusion.2
  (73 shorter events, 7.4 us)
Async XLA Ops:
  0.6 30.9 %collective-permute-start.1 = (bf16[121,1,1,128]{3,0,2,1:T(8,128)(2,1)}, bf16[121,1,1,128]{3,0,2,1:T(8,128)(2,1)S(1)}, u32[]{:S(2)}, u32[]{:S(2)}) collective-permute-start(bf16[121,1,1,128]{3,0,2,1:T(8,128)(2,1)} %bitcast.73), channel_id=1, source_target_pairs={{4,0},{8,4},{12,8},{16,12},{20,16},{24,20},{28,24},{0,28},{5,1},{9... | collective-permute-start | bytes 92936 | tf_op jit(solution)/shard_map/ppermute | solution.py:16
  6.7 24.8 %collective-permute-start = (bf16[121,1,1,128]{3,0,2,1:T(8,128)(2,1)}, bf16[121,1,1,128]{3,0,2,1:T(8,128)(2,1)S(1)}, u32[]{:S(2)}, u32[]{:S(2)}) collective-permute-start(bf16[121,1,1,128]{3,0,2,1:T(8,128)(2,1)} %bitcast.74), channel_id=1, source_target_pairs={{0,4},{4,8},{8,12},{12,16},{16,20},{20,24},{24,28},{28,0},{1,5},{5... | collective-permute-start | bytes 92936 | tf_op jit(solution)/shard_map/ppermute | solution.py:13
  20.8 7.2 %collective-permute-start.4 = (s32[1,1,3,32]{3,2,1,0:T(4,128)S(1)}, s32[1,1,3,32]{3,2,1,0:T(4,128)S(1)}, u32[]{:S(2)}, u32[]{:S(2)}) collective-permute-start(s32[1,1,3,32]{3,2,1,0:T(4,128)S(1)} %get-tuple-element.29), channel_id=1, source_target_pairs={{0,4},{4,8},{8,12},{12,16},{16,20},{20,24},{24,28},{28,0},{1,5},{5... | collective-permute-start | bytes 1160 | tf_op jit(solution)/shard_map/ppermute | solution.py:13
  20.8 7.2 %collective-permute-start.5 = (s32[1,1,3,32]{3,2,1,0:T(4,128)S(1)}, s32[1,1,3,32]{3,2,1,0:T(4,128)S(1)}, u32[]{:S(2)}, u32[]{:S(2)}) collective-permute-start(s32[1,1,3,32]{3,2,1,0:T(4,128)S(1)} %get-tuple-element.28), channel_id=1, source_target_pairs={{4,0},{8,4},{12,8},{16,12},{20,16},{24,20},{28,24},{0,28},{5,1},{9... | collective-permute-start | bytes 1160 | tf_op jit(solution)/shard_map/ppermute | solution.py:16
  28.1 1.5 collective-permute-start.7
  28.2 3.0 %collective-permute-start.6 = (s32[1,5,1,32]{3,2,1,0:T(1,128)S(1)}, s32[1,5,1,32]{3,2,1,0:T(1,128)S(1)}, u32[]{:S(2)}, u32[]{:S(2)}) collective-permute-start(s32[1,5,1,32]{3,2,1,0:T(1,128)S(1)} %get-tuple-element.24), channel_id=1, source_target_pairs={{0,1},{1,2},{2,3},{3,0},{4,5},{5,6},{6,7},{7,4},{8,9},{9,10},{10,1... | collective-permute-start | bytes 1928 | tf_op jit(solution)/shard_map/ppermute | solution.py:13
  32.3 2.3 %collective-permute-start.3 = (bf16[121,3,1,128]{3,0,2,1:T(8,128)(2,1)S(1)}, bf16[121,3,1,128]{3,0,2,1:T(8,128)(2,1)S(1)}, u32[]{:S(2)}, u32[]{:S(2)}) collective-permute-start(bf16[121,3,1,128]{3,0,2,1:T(8,128)(2,1)S(1)} %pad_maximum_fusion.3), channel_id=1, source_target_pairs={{1,0},{2,1},{3,2},{0,3},{5,4},{6,5},{7,6},{4,7},{9,8},{10,9},{11,1... | collective-permute-start | bytes 278792 | tf_op jit(solution)/shard_map/ppermute | solution.py:16
  32.4 5.1 %collective-permute-start.2 = (bf16[121,3,1,128]{3,0,2,1:T(8,128)(2,1)S(1)}, bf16[121,3,1,128]{3,0,2,1:T(8,128)(2,1)S(1)}, u32[]{:S(2)}, u32[]{:S(2)}) collective-permute-start(bf16[121,3,1,128]{3,0,2,1:T(8,128)(2,1)S(1)} %pad_maximum_fusion.3), channel_id=1, source_target_pairs={{0,1},{1,2},{2,3},{3,0},{4,5},{5,6},{6,7},{7,4},{8,9},{9,10},{10,1... | collective-permute-start | bytes 278792 | tf_op jit(solution)/shard_map/ppermute | solution.py:13
  119.6 21.9 %copy-start.1 = (s32[2048]{0:T(1024)S(1)}, s32[2048]{0:T(1024)}, u32[]{:S(2)}) copy-start(s32[2048]{0:T(1024)} %param.13) | copy-start | bytes 24580
  137.9 5.2 %collective-permute-start.9 = (bf16[121,1,3,32]{0,3,2,1:T(8,128)(2,1)S(1)}, bf16[121,1,3,32]{0,3,2,1:T(8,128)(2,1)S(1)}, u32[]{:S(2)}, u32[]{:S(2)}) collective-permute-start(bf16[121,1,3,32]{0,3,2,1:T(8,128)(2,1)S(1)} %get-tuple-element.21), channel_id=1, source_target_pairs={{4,0},{8,4},{12,8},{16,12},{20,16},{24,20},{28,24},{0,28},{5,1},{9... | collective-permute-start | bytes 69704 | tf_op jit(solution)/shard_map/ppermute | solution.py:16
  141.6 6.5 %collective-permute-start.8 = (bf16[121,1,3,32]{0,3,2,1:T(8,128)(2,1)S(1)}, bf16[121,1,3,32]{0,3,2,1:T(8,128)(2,1)S(1)}, u32[]{:S(2)}, u32[]{:S(2)}) collective-permute-start(bf16[121,1,3,32]{0,3,2,1:T(8,128)(2,1)S(1)} %get-tuple-element.20), channel_id=1, source_target_pairs={{0,4},{4,8},{8,12},{12,16},{16,20},{20,24},{24,28},{28,0},{1,5},{5... | collective-permute-start | bytes 69704 | tf_op jit(solution)/shard_map/ppermute | solution.py:13
  148.1 6.8 %collective-permute-start.11 = (bf16[121,5,1,32]{0,3,2,1:T(8,128)(2,1)S(1)}, bf16[121,5,1,32]{0,3,2,1:T(8,128)(2,1)S(1)}, u32[]{:S(2)}, u32[]{:S(2)}) collective-permute-start(bf16[121,5,1,32]{0,3,2,1:T(8,128)(2,1)S(1)} %get-tuple-element.17), channel_id=1, source_target_pairs={{1,0},{2,1},{3,2},{0,3},{5,4},{6,5},{7,6},{4,7},{9,8},{10,9},{11,1... | collective-permute-start | bytes 116168 | tf_op jit(solution)/shard_map/ppermute | solution.py:16
  148.2 6.7 %collective-permute-start.10 = (bf16[121,5,1,32]{0,3,2,1:T(8,128)(2,1)S(1)}, bf16[121,5,1,32]{0,3,2,1:T(8,128)(2,1)S(1)}, u32[]{:S(2)}, u32[]{:S(2)}) collective-permute-start(bf16[121,5,1,32]{0,3,2,1:T(8,128)(2,1)S(1)} %get-tuple-element.16), channel_id=1, source_target_pairs={{0,1},{1,2},{2,3},{3,0},{4,5},{5,6},{6,7},{7,4},{8,9},{9,10},{10,1... | collective-permute-start | bytes 116168 | tf_op jit(solution)/shard_map/ppermute | solution.py:13
  165.3 29.5 %copy-start = (f32[2048,4]{0,1:T(4,128)}, f32[2048,4]{0,1:T(4,128)S(1)}, u32[]{:S(2)}) copy-start(f32[2048,4]{0,1:T(4,128)S(1)} %multiply_reduce_fusion) | copy-start | bytes 98308
  171.6 3.8 %collective-permute-start.13 = (f32[9,1,3,32]{3,2,1,0:T(4,128)S(1)}, f32[9,1,3,32]{3,2,1,0:T(4,128)S(1)}, u32[]{:S(2)}, u32[]{:S(2)}) collective-permute-start(f32[9,1,3,32]{3,2,1,0:T(4,128)S(1)} %get-tuple-element.23), channel_id=1, source_target_pairs={{4,0},{8,4},{12,8},{16,12},{20,16},{24,20},{28,24},{0,28},{5,1},{9... | collective-permute-start | bytes 10376 | tf_op jit(solution)/shard_map/ppermute | solution.py:16
  171.7 6.5 %collective-permute-start.12 = (f32[9,1,3,32]{3,2,1,0:T(4,128)S(1)}, f32[9,1,3,32]{3,2,1,0:T(4,128)S(1)}, u32[]{:S(2)}, u32[]{:S(2)}) collective-permute-start(f32[9,1,3,32]{3,2,1,0:T(4,128)S(1)} %get-tuple-element.22), channel_id=1, source_target_pairs={{0,4},{4,8},{8,12},{12,16},{16,20},{20,24},{24,28},{28,0},{1,5},{5... | collective-permute-start | bytes 10376 | tf_op jit(solution)/shard_map/ppermute | solution.py:13
  178.2 12.8 %collective-permute-start.15 = (f32[9,5,1,32]{3,2,1,0:T(1,128)S(1)}, f32[9,5,1,32]{3,2,1,0:T(1,128)S(1)}, u32[]{:S(2)}, u32[]{:S(2)}) collective-permute-start(f32[9,5,1,32]{3,2,1,0:T(1,128)S(1)} %get-tuple-element.19), channel_id=1, source_target_pairs={{1,0},{2,1},{3,2},{0,3},{5,4},{6,5},{7,6},{4,7},{9,8},{10,9},{11,1... | collective-permute-start | bytes 17288 | tf_op jit(solution)/shard_map/ppermute | solution.py:16
  178.8 12.2 %collective-permute-start.14 = (f32[9,5,1,32]{3,2,1,0:T(1,128)S(1)}, f32[9,5,1,32]{3,2,1,0:T(1,128)S(1)}, u32[]{:S(2)}, u32[]{:S(2)}) collective-permute-start(f32[9,5,1,32]{3,2,1,0:T(1,128)S(1)} %get-tuple-element.18), channel_id=1, source_target_pairs={{0,1},{1,2},{2,3},{3,0},{4,5},{5,6},{6,7},{7,4},{8,9},{9,10},{10,1... | collective-permute-start | bytes 17288 | tf_op jit(solution)/shard_map/ppermute | solution.py:13
where the time goes:
time: 196 us; the launch traced here: 195 us
  local copies, waits for them, and re-layouts  113 us (58%)
  other arithmetic  27.6 us (14%)
  starting transfers between devices  18.8 us (10%)
  waiting for transfers between devices  17.2 us (9%)
  matrix products  16.7 us (9%)
    gather x1, local copies, waits for them, and re-layouts, shards(): gathered = jnp.take(columns, entries, axis=1)  81.1 us
    dot_general x1, matrix products, shards(): jnp.einsum('kqp,pkt->qt', translation_ops, gathered, preferred_element_ty...  16.7 us
    ppermute x8, starting transfers between devices, extended_2(): lax.ppermute(lax.slice_in_dim(block, 0, width, axis=dim), axis, backward)  15.4 us
    scatter x3, local copies, waits for them, and re-layouts, scatter_cols(): return start.at[:, place].set(source_box_index)[:, :incoming_row_data]  13.9 us
    scatter-add x2, other arithmetic, box_sums(): jax.ops.segment_sum(virial_terms.T, safe_slots, num_segments=capacity + 1)  13.2 us
    ppermute x8, waiting for transfers between devices, extended_2(): lax.ppermute(lax.slice_in_dim(block, block.shape[dim] - width, None, axis...  12.2 us
    gather x1, local copies, waits for them, and re-layouts, shards(): far_cols = jnp.take(returned, place, axis=1)  6.18 us
    gather x1, local copies, waits for them, and re-layouts, shards(): own_cols = jnp.take(padded_local, atom_slot, axis=1)  6.17 us
  transfers between devices with their start and end apart: 16, of which 7 were waited for; matrix products, arithmetic and copies ran while one was open for 19% of the time, Pallas kernels for 0%

commit v1 on v0

v1 whole, which is shorter than its diff:
```python
import functools

import jax
import jax.numpy as jnp
from jax import lax
from jax.experimental import pallas as pl
from jax.experimental.pallas import tpu as pltpu
from jax.sharding import PartitionSpec as P

BF = jnp.bfloat16
F32 = jnp.float32
REACH = 3
NSHIFT = 2 * REACH + 1
LANES = 128
BX = 4
BY = 4
BZ = 8
EXT = BX + 2 * REACH
SLAB_X = REACH * BY * BZ
SLAB_Y = BX * REACH * BZ + 2 * REACH * REACH * BZ
FIELDS = 4
STEP = 40
AROUND = [(1, 1), (1, 0), (1, 2), (2, 1), (2, 0), (2, 2), (0, 1), (0, 2)]
SENDERS = [(0, 1), (1, 1), (2, 1), (0, 2), (1, 2), (2, 2), (1, 0), (2, 0)]


def offsets():
    listed = []
    for dx in range(-REACH, REACH + 1):
        for dy in range(-REACH, REACH + 1):
            for dz in range(-REACH, REACH + 1):
                if max(abs(dx), abs(dy), abs(dz)) >= 2:
                    listed.append((dx, dy, dz))
    return listed


def up(value, unit):
    return -(-value // unit) * unit


def by_operator_kernel(first, ops_ref, out_ref, held, sems):
    terms, noff, _ = ops_ref.shape
    total = out_ref.shape[0]
    part = up(total // 4, 16)
    cuts = [slice(k, min(k + part, noff)) for k in range(0, noff, part)]
    copies = {}
    for j in range(held.shape[0]):
        q = (first + j) * 16
        some = min(16, terms - q)
        for n, cut in enumerate(cuts if j == 0 else [slice(0, noff)]):
            copies[j, cut.start] = pltpu.make_async_copy(
                ops_ref.at[q : q + some, cut, :], held.at[j, :some, cut, :], sems.at[n if j == 0 else j + len(cuts) - 1]
            )
            copies[j, cut.start].start()
    for j in range(held.shape[0]):
        some = min(16, terms - (first + j) * 16)
        rows = slice(16 * j, 16 * j + 16)
        for k0 in range(0, total, 16):
            if (j, k0) in copies:
                copies[j, k0].wait()
            x = held[j, :some, k0 : min(k0 + 16, noff), :]
            if k0 + 16 > noff:
                x = jnp.concatenate([x.astype(F32), jnp.zeros((some, k0 + 16 - noff, terms), F32)], axis=1).astype(BF)
            if some < 16:
                x = jnp.concatenate([x, jnp.zeros((16 - some, 16, terms), BF)], axis=0)
            x = jnp.swapaxes(x, 0, 1)
            x = jnp.concatenate([x, jnp.zeros((16, 16, LANES - terms), BF)], axis=2)
            out_ref[k0 : k0 + 16, rows, :] = x


def by_operator(ops, first, steps):
    noff, terms, _ = ops.shape
    total = up(noff, 16)
    return pl.pallas_call(
        functools.partial(by_operator_kernel, first),
        in_specs=[pl.BlockSpec(memory_space=pl.ANY)],
        out_specs=pl.BlockSpec(memory_space=pltpu.VMEM),
        out_shape=pltpu.VMEM((total, steps * 16, LANES), BF),
        scratch_shapes=[pltpu.VMEM((steps, 16, noff, terms), BF), pltpu.SemaphoreType.DMA((steps + 3,))],
        compiler_params=pltpu.CompilerParams(vmem_limit_bytes=16 * 2**20),
        cost_estimate=pl.CostEstimate(flops=0, bytes_accessed=2 * total * steps * 16 * LANES * 2, transcendentals=0),
        name="by_operator",
    )(pltpu.with_memory_space_constraint(jnp.transpose(ops, (1, 0, 2)), pltpu.HBM))


INNER = [(3, None), (4, None), (5, None), (2, 1), (6, 0)]
OUTER = [(1, None), (2, None), (6, None), (7, None), (0, 1), (8, 0)]


def shift_sources(pairs, grid, out_ref):
    parity = lax.broadcasted_iota(jnp.int32, (BZ, LANES), 0) % 2
    nothing = jnp.zeros((BZ, LANES), F32)
    for dz in range(-REACH, REACH + 1):
        for x in range(EXT):
            turned = {}

            def tile(y):
                if y not in turned:
                    t = grid[x, y]
                    if dz:
                        t = pltpu.roll(t, (-dz) % BZ, 0)
                    if abs(dz) == REACH:
                        t = jnp.where(parity == (0 if dz > 0 else 1), t, 0.0)
                    turned[y] = t
                return turned[y]

            for n, (y, keep) in enumerate(pairs):
                halves = [tile(y + i) if keep in (None, i) else nothing for i in range(2)]
                out_ref[((dz + REACH) * len(pairs) + n) * EXT + x] = jnp.concatenate(halves, axis=0).astype(BF)


def shifted_sources(inner, outer, offset):
    dx, dy, dz = offset
    tiles = []
    for bx in range(BX):
        for h in range(2):
            pair = (dy + REACH + 2 * h, {-REACH: 1, REACH: 0}.get(dy))
            ref, pairs = (inner, INNER) if pair in INNER else (outer, OUTER)
            if abs(dx) == REACH and bx % 2 != (0 if dx > 0 else 1):
                tiles.append(jnp.zeros((16, LANES), BF))
            else:
                tiles.append(ref[((dz + REACH) * len(pairs) + pairs.index(pair)) * EXT + REACH + dx + bx])
    return jnp.concatenate(tiles, axis=0)


def one_hot(index, rows):
    at = lax.broadcasted_iota(jnp.int32, (rows, index.shape[1]), 0)
    return (at == index).astype(F32).astype(BF)


def split3(x):
    high = x.astype(BF).astype(F32)
    middle = (x - high).astype(BF).astype(F32)
    return jnp.concatenate([high, middle, x - high - middle], axis=0).astype(BF)


def nt(a, b):
    return lax.dot_general(a, b, (((1,), (1,)), ((), ())), preferred_element_type=F32)


def neighbours(size_x, size_y):
    ix, iy = lax.axis_index("xs"), lax.axis_index("ys")
    step_x = [0, 1 - 2 * lax.rem(ix, 2), 2 * lax.rem(ix, 2) - 1]
    step_y = [0, 1 - 2 * lax.rem(iy, 2), 2 * lax.rem(iy, 2) - 1]
    return [
        lax.rem(ix + step_x[x] + size_x, size_x) * size_y + lax.rem(iy + step_y[y] + size_y, size_y)
        for x, y in AROUND
    ]


def pack_kernel(sizes, owner_hbm, slot_hbm, table_hbm, multipoles_hbm, evaluation_ref, ion_hbm,
                own_ref, x_even_ref, x_odd_ref, y_even_ref, y_odd_ref, rows_ref, place_ref,
                held, owner_ref, slot_ref, table_ref, multipoles_ref, ion_ref, sems):
    terms = multipoles_ref.shape[0]
    groups = held.shape[0]
    above = offsets().index((0, 0, 2))
    small = [(table_hbm.at[above // 8 * 8 : above // 8 * 8 + 8, :], table_ref), (multipoles_hbm, multipoles_ref),
             (owner_hbm, owner_ref), (slot_hbm, slot_ref), (ion_hbm, ion_ref)]
    copies = [pltpu.make_async_copy(evaluation_ref.at[:, 16 * j : 16 * j + 16, :], held.at[j], sems.at[j])
              for j in range(groups)]
    copies += [pltpu.make_async_copy(a, b, sems.at[groups + i]) for i, (a, b) in enumerate(small)]
    for copy in copies[groups:] + copies[:groups]:
        copy.start()
    for copy in copies[groups:]:
        copy.wait()
    chunks = slot_ref.shape[0]
    per_peer = place_ref.shape[0] // 8
    row = table_ref[above % 8 : above % 8 + 1, :]
    z = lax.broadcasted_iota(jnp.int32, row.shape, 1) % BZ
    row = jnp.where(z >= 2, pltpu.roll(row, 2, 1), pltpu.roll(row, LANES - 6, 1))
    masked = jnp.where(row >= 0, multipoles_ref[...].astype(F32), 0.0)
    masked = jnp.concatenate([masked, jnp.zeros((LANES - terms, LANES), F32)], axis=0).T
    own_ref[...] = masked.astype(BF)
    even_x = lax.rem(lax.axis_index("xs"), 2) == 0
    lower, upper = masked[:SLAB_X], masked[LANES - SLAB_X :]
    x_even_ref[:SLAB_X] = jnp.where(even_x, upper, lower).astype(BF)
    x_odd_ref[:SLAB_X] = jnp.where(even_x, lower, upper).astype(BF)

    owner = owner_ref[...]
    member = [(owner == device).astype(F32) for device in neighbours(*sizes)]
    stacked = jnp.concatenate(member, axis=0).astype(BF)
    n = 8 * chunks
    r = lax.broadcasted_iota(jnp.int32, (n, n), 0)
    c = lax.broadcasted_iota(jnp.int32, (n, n), 1)
    earlier = ((r // chunks == c // chunks) & (c < r)).astype(F32).astype(BF)
    r = lax.broadcasted_iota(jnp.int32, (LANES, LANES), 0)
    c = lax.broadcasted_iota(jnp.int32, (LANES, LANES), 1)
    before = (r < c).astype(F32).astype(BF)
    ones = jnp.ones((LANES, LANES), BF)
    ahead = jnp.dot(earlier, stacked, preferred_element_type=F32).astype(BF)
    rank = jnp.dot(stacked, before, preferred_element_type=F32) + jnp.dot(ahead, ones, preferred_element_type=F32)
    place = jnp.full((chunks, LANES), -1.0, F32)
    for d in range(8):
        place = jnp.where(member[d] > 0, rank[d * chunks : (d + 1) * chunks] + d * per_peer, place)
    place = place.astype(jnp.int32)
    for j in range(chunks):
        place_ref[:, j * LANES : (j + 1) * LANES] = one_hot(place[j : j + 1], 8 * per_peer)

    half_way = groups // 2 * 4 * LANES

    def picked_by(first, last):
        x = rows_ref[:, :, first:last].reshape(FIELDS * LANES, last - first)
        return nt(x, place_ref[:, first:last])

    slot = slot_ref[...].astype(F32)
    for j in range(chunks // 4):
        part = slice(16 * j, 16 * j + 16)
        if j == groups // 2:
            picked = picked_by(0, half_way)
        slots = [jnp.broadcast_to(slot[4 * j + i : 4 * j + i + 1], (4, LANES)) for i in range(4)]
        extra = [ion_ref[part, :], jnp.concatenate(slots, axis=0).astype(BF)]
        extra = jnp.concatenate([e.reshape(1, 16, LANES) for e in extra], axis=0)
        copies[j].wait()
        for p in range(0, LANES, 16):
            x = held[j, p : min(p + 16, terms)]
            if p + 16 > terms:
                x = jnp.concatenate([x, extra, jnp.zeros((16 - x.shape[0] - 2, 16, LANES), BF)], axis=0)
            x = jnp.swapaxes(x, 0, 1)
            for i in range(4):
                lanes = slice((4 * j + i) * LANES, (4 * j + i + 1) * LANES)
                for f in range(FIELDS):
                    rows_ref[f, p : p + 16, lanes] = x[4 * i + f]

    picked = picked + picked_by(half_way, place_ref.shape[1])

    targets = {
        (1, 1): (x_even_ref, 0), (1, 0): (x_even_ref, 1), (1, 2): (x_even_ref, 2),
        (2, 1): (x_odd_ref, 0), (2, 0): (x_odd_ref, 1), (2, 2): (x_odd_ref, 2),
        (0, 1): (y_even_ref, 0), (0, 2): (y_odd_ref, 0),
    }
    lane = lax.broadcasted_iota(jnp.int32, (LANES, LANES), 1) // per_peer
    each = LANES // per_peer
    turned = []
    for half in range(2):
        x = [picked[f * LANES : (f + 1) * LANES, half * LANES : (half + 1) * LANES] for f in range(FIELDS)]
        turned.append([pltpu.roll(t, f * per_peer, 1) if f else t for f, t in enumerate(x)])
    for d, where in enumerate(AROUND):
        message = turned[d // each][0]
        for f in range(1, FIELDS):
            message = jnp.where(lane == (f + d) % each, turned[d // each][f], message)
        ref, at = targets[where]
        at = at * LANES + (SLAB_X if where[0] else 0)
        ref[at : at + LANES] = message.astype(BF)


def pack(sizes, owner, slot, table, multipoles, evaluation, ions):
    terms = multipoles.shape[0]
    atoms = slot.shape[0]
    chunks = atoms // LANES
    per_peer = atoms // 64
    whole = pl.BlockSpec(memory_space=pltpu.VMEM)
    view = evaluation.transpose(1, 0, 2).reshape(terms, FIELDS, chunks, LANES)
    view = view.transpose(0, 2, 1, 3).reshape(terms, FIELDS * chunks, LANES)
    ions = ions.reshape(FIELDS, chunks, LANES).transpose(1, 0, 2).reshape(FIELDS * chunks, LANES)
    block = lambda rows: jax.ShapeDtypeStruct((rows, LANES), BF)
    return pl.pallas_call(
        functools.partial(pack_kernel, sizes),
        in_specs=[pl.BlockSpec(memory_space=pl.ANY)] * 6,
        out_specs=[whole] * 7,
        out_shape=[block(LANES), block(SLAB_X + 3 * LANES), block(SLAB_X + 3 * LANES), block(LANES), block(LANES),
                   pltpu.VMEM((FIELDS, LANES, atoms), BF),
                   pltpu.VMEM((8 * per_peer, atoms), BF)],
        scratch_shapes=[
            pltpu.VMEM((chunks // 4, terms, 16, LANES), BF),
            pltpu.VMEM((chunks, LANES), jnp.int32),
            pltpu.VMEM((chunks, LANES), jnp.int32),
            pltpu.VMEM((8, LANES), jnp.int32),
            pltpu.VMEM((terms, LANES), BF),
            pltpu.VMEM((FIELDS * chunks, LANES), BF),
            pltpu.SemaphoreType.DMA((chunks // 4 + 5,)),
        ],
        compiler_params=pltpu.CompilerParams(vmem_limit_bytes=24 * 2**20),
        name="pack",
    )(*(pltpu.with_memory_space_constraint(x, pltpu.HBM) for x in (
        owner.reshape(chunks, LANES), slot.reshape(chunks, LANES), table, multipoles, view, ions)))


def tiles_of(ref, first, shape):
    nx, ny = shape
    value = ref[first : first + nx * ny * BZ, :].astype(F32)
    return {(x, y): value[(x * ny + y) * BZ : (x * ny + y + 1) * BZ] for x in range(nx) for y in range(ny)}


def forward_kernel(own, x_even, x_odd, y_even_message, y_odd_message, y_even_ref, y_odd_ref, even_messages_ref, odd_messages_ref):
    even_y = lax.rem(lax.axis_index("ys"), 2) == 0
    lower, upper = [], []
    for ref, nx in ((own, BX), (x_even, REACH), (x_odd, REACH)):
        tiles = tiles_of(ref, 0, (nx, BY))
        lower += [tiles[x, y] for x in range(nx) for y in range(REACH)]
        upper += [tiles[x, y + BY - REACH] for x in range(nx) for y in range(REACH)]
    lower, upper = jnp.concatenate(lower, axis=0), jnp.concatenate(upper, axis=0)
    y_even_ref[:SLAB_Y] = jnp.where(even_y, upper, lower).astype(BF)
    y_odd_ref[:SLAB_Y] = jnp.where(even_y, lower, upper).astype(BF)
    y_even_ref[SLAB_Y:] = y_even_message[...]
    y_odd_ref[SLAB_Y:] = y_odd_message[...]
    for ref, at in ((even_messages_ref, 0), (odd_messages_ref, 2)):
        for i, source in enumerate((x_even, x_odd)):
            first = SLAB_X + at * LANES
            ref[i * LANES : (i + 1) * LANES] = source[first : first + LANES]


def forward(*operands):
    vmem = pl.BlockSpec(memory_space=pltpu.VMEM)
    return pl.pallas_call(
        forward_kernel,
        in_specs=[vmem] * 5,
        out_specs=[vmem] * 4,
        out_shape=[pltpu.VMEM((SLAB_Y + LANES, LANES), BF)] * 2 + [pltpu.VMEM((2 * LANES, LANES), BF)] * 2,
        compiler_params=pltpu.CompilerParams(vmem_limit_bytes=4 * 2**20),
        name="forward",
    )(*operands)


def sources_along_x(own, x_even, x_odd):
    even_x = lax.rem(lax.axis_index("xs"), 2) == 0
    found = {(REACH + x, REACH + y): t for (x, y), t in tiles_of(own, 0, (BX, BY)).items()}
    a, b = tiles_of(x_even, 0, (REACH, BY)), tiles_of(x_odd, 0, (REACH, BY))
    for x, y in a:
        found[x, REACH + y] = jnp.where(even_x, b[x, y], a[x, y])
        found[REACH + BX + x, REACH + y] = jnp.where(even_x, a[x, y], b[x, y])
    return found


def sources_along_y(y_even, y_odd):
    even_x = lax.rem(lax.axis_index("xs"), 2) == 0
    even_y = lax.rem(lax.axis_index("ys"), 2) == 0
    strips = []
    for ref in (y_even, y_odd):
        strip = {(REACH + x, y): t for (x, y), t in tiles_of(ref, 0, (BX, REACH)).items()}
        first = BX * REACH * BZ
        a = tiles_of(ref, first, (REACH, REACH))
        b = tiles_of(ref, first + REACH * REACH * BZ, (REACH, REACH))
        for x, y in a:
            strip[x, y] = jnp.where(even_x, b[x, y], a[x, y])
            strip[REACH + BX + x, y] = jnp.where(even_x, a[x, y], b[x, y])
        strips.append(strip)
    found = {}
    for x, y in strips[0]:
        found[x, y] = jnp.where(even_y, strips[1][x, y], strips[0][x, y])
        found[x, REACH + BY + y] = jnp.where(even_y, strips[0][x, y], strips[1][x, y])
    return found


def inner_kernel(own, x_even, x_odd, shifted_ref, grid_ref):
    for (x, y), box in sources_along_x(own, x_even, x_odd).items():
        grid_ref[x, y] = box
    shift_sources(INNER, grid_ref, shifted_ref)


def inner_pairs(own, x_even, x_odd):
    vmem = pl.BlockSpec(memory_space=pltpu.VMEM)
    return pl.pallas_call(
        inner_kernel,
        in_specs=[vmem] * 3,
        out_specs=[vmem] * 2,
        out_shape=[pltpu.VMEM((NSHIFT * len(INNER) * EXT, 16, LANES), BF), pltpu.VMEM((EXT, REACH + BY, BZ, LANES), F32)],
        compiler_params=pltpu.CompilerParams(vmem_limit_bytes=8 * 2**20),
        cost_estimate=pl.CostEstimate(flops=0, bytes_accessed=3 * 2**20, transcendentals=0),
        name="inner_pairs",
    )(own, x_even, x_odd)


def messages(x_even, x_odd, y_even, y_odd, even_passed, odd_passed):
    along_y = []
    for direct, passed in ((y_even, even_passed), (y_odd, odd_passed)):
        along_y += [(direct, SLAB_Y), (passed, 0), (passed, LANES)]
    return along_y + [(x_even, SLAB_X + LANES), (x_odd, SLAB_X + LANES)]


def m2l_kernel(inner, along_x, y_odd, y_even, first_ref, second_ref, local_ref, grid, outer):
    for (x, y), box in sources_along_y(y_even, y_odd).items():
        grid[x, y] = box
    for x in range(EXT):
        for y in (REACH, REACH + BY - 1):
            grid[x, y] = along_x[x, y]
    shift_sources(OUTER, grid, outer)
    listed = offsets()
    acc = jnp.zeros((LANES, LANES), F32)
    for k0 in range(0, len(listed), STEP):
        some = range(k0, min(k0 + STEP, len(listed)))
        a = [jnp.concatenate([first_ref[k], second_ref[k]], axis=0) for k in some]
        b = [shifted_sources(inner, outer, listed[k]) for k in some]
        acc = acc + nt(jnp.concatenate(a, axis=1), jnp.concatenate(b, axis=1))
    local_ref[...] = acc.astype(BF)


def m2l(inner, along_x, y_odd, y_even, first, second):
    vmem = pl.BlockSpec(memory_space=pltpu.VMEM)
    pinned = [pltpu.with_memory_space_constraint(x, pltpu.VMEM) for x in (inner, along_x, first, second)]
    return pl.pallas_call(
        m2l_kernel,
        in_specs=[vmem] * 6,
        out_specs=vmem,
        out_shape=jax.ShapeDtypeStruct((LANES, LANES), BF),
        scratch_shapes=[
            pltpu.VMEM((EXT, EXT, BZ, LANES), F32),
            pltpu.VMEM((NSHIFT * len(OUTER) * EXT, 16, LANES), BF),
        ],
        compiler_params=pltpu.CompilerParams(vmem_limit_bytes=16 * 2**20),
        cost_estimate=pl.CostEstimate(flops=0, bytes_accessed=2**16, transcendentals=0),
        name="m2l",
    )(pinned[0], pinned[1], y_odd, y_even, pinned[2], pinned[3])


def answer_kernel(terms, local_ref, x_odd, x_even, y_odd, y_even, odd_passed, even_passed, down_ref, up_ref, side_ref, tail_ref):
    local = local_ref[...]
    row = lax.broadcasted_iota(jnp.int32, (8, LANES), 0)
    answers = []
    for i, (ref, at) in enumerate(messages(x_even, x_odd, y_even, y_odd, even_passed, odd_passed)):
        x = ref[at : at + LANES, :].astype(F32)
        tail_ref[i : i + 1] = x[terms : terms + 1]
        tail_ref[8 + i : 9 + i] = x[terms + 1 : terms + 2]
        spread = one_hot(x[terms + 1 : terms + 2].astype(jnp.int32), LANES)
        column = jnp.dot(local, spread, preferred_element_type=F32)
        answers.append(jnp.sum(x[:terms] * column[:terms], axis=0, keepdims=True))
    for ref, first in ((down_ref, 0), (up_ref, 3), (side_ref, 6)):
        tile = jnp.zeros((8, LANES), F32)
        for i in range(min(3, 8 - first)):
            tile = jnp.where(row == i, answers[first + i], tile)
        ref[...] = tile


def answer(terms, *operands):
    vmem = pl.BlockSpec(memory_space=pltpu.VMEM)
    return pl.pallas_call(
        functools.partial(answer_kernel, terms),
        in_specs=[vmem] * 7,
        out_specs=[vmem] * 4,
        out_shape=[jax.ShapeDtypeStruct((8, LANES), F32)] * 3 + [jax.ShapeDtypeStruct((16, LANES), F32)],
        compiler_params=pltpu.CompilerParams(vmem_limit_bytes=4 * 2**20),
        name="answer",
    )(*operands)


def atoms_kernel(size_y, owner_ref, slot_ref, ion_ref, rows_ref, local_ref, tail_ref,
                 down_ref, up_ref, side_ref, local_exp_ref, far_ref, virial_ref):
    chunks = slot_ref.shape[0]
    local = local_ref[...]
    local_exp_ref[...] = local[: local_exp_ref.shape[0]]
    slots = jnp.where(owner_ref[...] == lax.axis_index("xs") * size_y + lax.axis_index("ys"), slot_ref[...], -1)
    row = lax.broadcasted_iota(jnp.int32, (8, LANES), 0)
    total = jnp.zeros((9 * 8, LANES), F32)
    for j in range(chunks):
        lanes = slice(j * LANES, (j + 1) * LANES)
        spread = one_hot(slots[j : j + 1], LANES)
        column = jnp.dot(local, spread, preferred_element_type=F32)
        far = jnp.zeros((8, LANES), F32)
        for f in range(FIELDS):
            value = jnp.sum(rows_ref[f, :, lanes].astype(F32) * column, axis=0, keepdims=True)
            far = jnp.where(row == f, value, far)
        far_ref[:, lanes] = far[:FIELDS]
        ion = ion_ref[j * FIELDS : (j + 1) * FIELDS, :].astype(F32)
        terms3 = jnp.concatenate([ion[0:1] * ion[a : a + 1] * far for a in (1, 2, 3)], axis=0)
        total = total + nt(split3(terms3), spread)

    per_peer = side_ref.shape[1] // FIELDS
    group = lax.broadcasted_iota(jnp.int32, (8, LANES), 1) // per_peer
    answers = [(down_ref, 0), (down_ref, 1), (down_ref, 2), (up_ref, 0), (up_ref, 1), (up_ref, 2), (side_ref, 0), (side_ref, 1)]
    for n, (answer, i) in enumerate(answers):
        d = AROUND.index(SENDERS[n])
        spread = one_hot(tail_ref[8 + n : 9 + n].astype(jnp.int32), LANES)
        ion = jnp.broadcast_to(tail_ref[n : n + 1], (8, LANES))

        def everywhere(f):
            x = jnp.where(group == (f + d) % FIELDS, ion, 0.0)
            x = x + pltpu.roll(x, 2 * per_peer, 1)
            return x + pltpu.roll(x, per_peer, 1)

        far = jnp.where(group == (row + d) % FIELDS, jnp.broadcast_to(answer[i : i + 1, :], (8, LANES)), 0.0)
        charge = everywhere(0)
        terms3 = jnp.concatenate([charge * everywhere(a) * far for a in (1, 2, 3)], axis=0)
        total = total + nt(split3(terms3), spread)
    virial = total[:24] + total[24:48] + total[48:]
    for a in range(3):
        virial_ref[3 * a : 3 * a + 3, :] = virial[8 * a + 1 : 8 * a + 4]


def atoms_of_device(terms, size_y, owner, slot, ions, rows, local, tail, down, up_, side):
    atoms = slot.shape[0]
    chunks = atoms // LANES
    whole = pl.BlockSpec(memory_space=pltpu.VMEM)
    ions = ions.reshape(FIELDS, chunks, LANES).transpose(1, 0, 2).reshape(FIELDS * chunks, LANES)
    return pl.pallas_call(
        functools.partial(atoms_kernel, size_y),
        in_specs=[whole] * 9,
        out_specs=[whole] * 3,
        out_shape=[jax.ShapeDtypeStruct((terms, LANES), BF), jax.ShapeDtypeStruct((FIELDS, atoms), F32),
                   jax.ShapeDtypeStruct((9, LANES), F32)],
        compiler_params=pltpu.CompilerParams(vmem_limit_bytes=16 * 2**20),
        cost_estimate=pl.CostEstimate(flops=4 * 10**6, bytes_accessed=8 * 2**20, transcendentals=0),
        name="atoms",
    )(owner.reshape(chunks, LANES), slot.reshape(chunks, LANES), ions, pltpu.with_memory_space_constraint(rows, pltpu.VMEM), local, tail, down, up_, side)


def turn_kernel(answer_x, y_even, y_odd, x_odd_ref, x_even_ref):
    for n, ref in ((1, x_even_ref), (2, x_odd_ref)):
        ref[...] = jnp.zeros(ref.shape, F32)
        ref[0:1] = answer_x[n - 1 : n]
        ref[1:2] = y_odd[n : n + 1]
        ref[2:3] = y_even[n : n + 1]


def turn(*operands):
    vmem = pl.BlockSpec(memory_space=pltpu.VMEM)
    return pl.pallas_call(
        turn_kernel,
        in_specs=[vmem] * 3,
        out_specs=[vmem] * 2,
        out_shape=[jax.ShapeDtypeStruct((8, LANES), F32)] * 2,
        compiler_params=pltpu.CompilerParams(vmem_limit_bytes=2**20),
        name="turn",
    )(*operands)


def merge_kernel(far_ref, place_ref, x_odd, x_even, y_odd, y_even, out_ref):
    per_peer = place_ref.shape[0] // 8
    each = LANES // per_peer
    returned = {
        (0, 1): (y_even, 0), (0, 2): (y_odd, 0),
        (1, 0): (x_even, 0), (1, 2): (x_even, 1), (1, 1): (x_even, 2),
        (2, 0): (x_odd, 0), (2, 2): (x_odd, 1), (2, 1): (x_odd, 2),
    }
    row = lax.broadcasted_iota(jnp.int32, (8, LANES), 0)
    group = lax.broadcasted_iota(jnp.int32, (8, LANES), 1) // per_peer
    halves = []
    for half in range(2):
        x = []
        for where in AROUND[half * each : half * each + each]:
            ref, i = returned[where]
            x.append(jnp.broadcast_to(ref[i : i + 1, :], (8, LANES)))
        tile = jnp.zeros((8, LANES), F32)
        for f in range(FIELDS):
            y = x[0]
            for g in range(1, each):
                y = jnp.where(group == (f + g) % each, x[g], y)
            tile = jnp.where(row == f, pltpu.roll(y, (each - f) * per_peer, 1) if f else y, tile)
        halves.append(tile)
    back = split3(jnp.concatenate(halves, axis=1))
    added = jnp.dot(back, place_ref[...], preferred_element_type=F32)
    out_ref[...] = far_ref[...] + (added[:FIELDS] + added[8 : 8 + FIELDS] + added[16 : 16 + FIELDS])


def merge(far, place, *returned):
    whole = pl.BlockSpec(memory_space=pltpu.VMEM)
    return pl.pallas_call(
        merge_kernel,
        in_specs=[whole] * 6,
        out_specs=whole,
        out_shape=jax.ShapeDtypeStruct(far.shape, F32),
        compiler_params=pltpu.CompilerParams(vmem_limit_bytes=16 * 2**20),
        name="merge",
    )(far, pltpu.with_memory_space_constraint(place, pltpu.VMEM), *returned)


def across(axis, edge, block):
    count = lax.axis_size(axis)
    pairs = [(i, (i + 1) % count) for i in range(edge - 1, count, 2)]
    return lax.ppermute(block, axis, pairs + [(b, a) for a, b in pairs])


def shards(
    multipoles,
    translation_ops,
    target_interaction_table,
    evaluation,
    ion_data,
    atom_owner,
    atom_slot,
):
    num_terms = multipoles.shape[0]
    size_x = lax.axis_size("xs")
    size_y = lax.axis_size("ys")
    own, to_x_even, to_x_odd, y_even_message, y_odd_message, rows, place = pack(
        (size_x, size_y), atom_owner, atom_slot, target_interaction_table, multipoles, evaluation, ion_data
    )
    x_even = across("xs", 1, to_x_even)
    x_odd = across("xs", 2, to_x_odd)
    first = by_operator(translation_ops, 0, 6)
    x_even, x_odd, first = lax.optimization_barrier((x_even, x_odd, first))
    to_y_even, to_y_odd, even_messages, odd_messages = forward(own, x_even, x_odd, y_even_message, y_odd_message)
    y_odd = across("ys", 2, to_y_odd)
    y_even = across("ys", 1, to_y_even)
    odd_messages = across("ys", 2, odd_messages)
    even_messages = across("ys", 1, even_messages)
    second = by_operator(translation_ops, 6, 2)
    inner, along_x = inner_pairs(own, x_even, x_odd)
    local = m2l(inner, along_x, y_odd, y_even, first, second)
    answer_y_even, answer_y_odd, answer_x, tail = answer(
        num_terms, local, x_odd, x_even, y_odd, y_even, odd_messages, even_messages
    )

    back_y_odd = across("ys", 2, answer_y_odd)
    back_y_even = across("ys", 1, answer_y_even)
    local_exp, far, box_virial = atoms_of_device(
        num_terms, size_y, atom_owner, atom_slot, ion_data, rows, local, tail, answer_y_even, answer_y_odd, answer_x
    )
    answer_x_odd, answer_x_even = turn(answer_x, back_y_even, back_y_odd)
    back_x_odd = across("xs", 2, answer_x_odd)
    back_x_even = across("xs", 1, answer_x_even)
    atom_far_field = merge(far, place, back_x_odd, back_x_even, back_y_odd, back_y_even)
    return (local_exp, atom_far_field, box_virial)


def solution(mesh):
    placed = (
        P(None, ("xs", "ys")),
        P(),
        P(None, ("xs", "ys")),
        P(None, None, ("xs", "ys")),
        P(None, ("xs", "ys")),
        P(("xs", "ys"), None),
        P(("xs", "ys")),
    )
    return jax.shard_map(
        shards,
        mesh=mesh,
        in_specs=placed,
        out_specs=(P(None, ("xs", "ys")), P(None, ("xs", "ys")), P(None, ("xs", "ys"))),
        check_vma=False,
    )
```

time: 196 us -> 34.1 us (0.17)
  local copies, waits for them, and re-layouts: 113 us -> 0.01 us
  other arithmetic: 27.6 us -> 0 us
  matrix products: 16.7 us -> 0 us
  Pallas kernels: 0 us -> 16.7 us
  waiting for transfers between devices: 17.2 us -> 2.99 us
  starting transfers between devices: 18.8 us -> 13.5 us
    gather x4 -> x0, local copies, waits for them, and re-layouts: 94.8 us -> none  [the longest x1 81.1 us: shards(): gathered = jnp.take(columns, entries, axis=1)]
    pallas_call x0 -> x10, Pallas kernels: none -> 16.7 us  [the longest x2 6.72 us: by_operator(): pl.pallas_call(functools.partial(by_operator_kernel, first), in_specs=[pl...]
    dot_general x1 -> x0, matrix products: 16.7 us -> none  [shards(): jnp.einsum('kqp,pkt->qt', translation_ops, gathered, preferred_element_ty...]
    ppermute x16 -> x10, waiting for transfers between devices: 17.2 us -> 2.99 us  [across(): return lax.ppermute(block, axis, pairs + [(b, a) for a, b in pairs])]
    scatter x3 -> x0, local copies, waits for them, and re-layouts: 13.9 us -> none  [scatter_cols(): return start.at[:, place].set(source_box_index)[:, :incoming_row_data]]
    scatter-add x2 -> x0, other arithmetic: 13.2 us -> none  [box_sums(): jax.ops.segment_sum(virial_terms.T, safe_slots, num_segments=capacity + 1)]
    ppermute x16 -> x10, starting transfers between devices: 18.8 us -> 13.5 us  [across(): return lax.ppermute(block, axis, pairs + [(b, a) for a, b in pairs])]
    another operation x3 -> x0, other arithmetic: 2.82 us -> none
  transfers between devices with their start and end apart: 16 -> 10, of which waited for: 7 -> 4; matrix products, arithmetic and copies ran while one was open for 19% -> 0% of each run, Pallas kernels for 0% -> 37%
where the time goes in v1:
time: 34.1 us; the launch traced here: 34 us
  Pallas kernels  16.7 us (49%)
  starting transfers between devices  13.5 us (40%)
  waiting for transfers between devices  2.99 us (9%)
  between operations  0.74 us (2%)
    ppermute x10, starting transfers between devices, across(): return lax.ppermute(block, axis, pairs + [(b, a) for a, b in pairs])  13.5 us
    pallas_call x2, Pallas kernels, by_operator(): pl.pallas_call(functools.partial(by_operator_kernel, first), in_specs=[pl...  6.72 us
    pallas_call x1, Pallas kernels, pack(): pl.pallas_call(functools.partial(pack_kernel, sizes), in_specs=[pl.BlockS...  3.05 us
    ppermute x10, waiting for transfers between devices, across(): return lax.ppermute(block, axis, pairs + [(b, a) for a, b in pairs])  2.99 us
    pallas_call x1, Pallas kernels, m2l(): pl.pallas_call(m2l_kernel, in_specs=[vmem] * 6, out_specs=vmem, out_shape...  2.87 us
    pallas_call x1, Pallas kernels, atoms_of_device(): pl.pallas_call(functools.partial(atoms_kernel, size_y), in_specs=[whole]...  2.73 us
    pallas_call x1, Pallas kernels, merge(): pl.pallas_call(merge_kernel, in_specs=[whole] * 6, out_specs=whole, out_s...  0.96 us
  transfers between devices with their start and end apart: 10, of which 4 were waited for; matrix products, arithmetic and copies ran while one was open for 0% of the time, Pallas kernels for 37%

profile of v1, /device:TPU:0, one launch (start us, length us, event | category | flops | bytes accessed | tf_op | source)
XLA Modules:
  0.0 34.0 jit_solution(18206471575494899756)
XLA Ops:
  0.6 3.1 %pack.1 = (bf16[128,128]{1,0:T(8,128)(2,1)S(1)}, bf16[480,128]{1,0:T(8,128)(2,1)S(1)}, bf16[480,128]{1,0:T(8,128)(2,1)S(1)}, bf16[128,128]{1,0:T(8,128)(2,1)S(1)...) custom-call(s32[16,128]{1,0:T(8,128)} %bitcast.17, ...), custom_call_target="tpu_custom_call" | custom-call | tf_op jit(solution)/shard_map/pack/pallas_call | solution.py:256
  3.7 3.0 %collective-permute-start = (bf16[480,128]{1,0:T(8,128)(2,1)S(1)}, bf16[480,128]{1,0:T(8,128)(2,1)S(1)}, u32[]{:S(2)}, u32[]{:S(2)}) collective-permute-start(bf16[480,128]{1,0:T(8,128)(2,1)S(1)} %get-tuple-element.30), channel_id=1, source_target_pairs={{0,4},{8,12},{16,20},{24,28},{4,0},{12,8},{20,16},{28,24},{1,5},{9... | collective-permute-start | bytes 368648 | tf_op jit(solution)/shard_map/ppermute | solution.py:558
  6.7 3.5 %collective-permute-start.1 = (bf16[480,128]{1,0:T(8,128)(2,1)S(1)}, bf16[480,128]{1,0:T(8,128)(2,1)S(1)}, u32[]{:S(2)}, u32[]{:S(2)}) collective-permute-start(bf16[480,128]{1,0:T(8,128)(2,1)S(1)} %get-tuple-element.31), channel_id=1, source_target_pairs={{4,8},{12,16},{20,24},{28,0},{8,4},{16,12},{24,20},{0,28},{5,9},{1... | collective-permute-start | bytes 368648 | tf_op jit(solution)/shard_map/ppermute | solution.py:558
  10.3 4.6 %by_operator.2.first_ref = bf16[320,96,128]{2,1,0:T(8,128)(2,1)S(1)} custom-call(bf16[121,316,121]{2,1,0:T(8,128)(2,1)} %bitcast.21), custom_call_target="tpu_custom_call" | custom-call | bytes 15728640 | tf_op jit(solution)/shard_map/by_operator/pallas_call | solution.py:74
  14.9 0.0 collective-permute-done.x_even
  14.9 0.0 collective-permute-done.1.x_odd
  15.0 0.4 %collective-permute-start.2 = (bf16[368,128]{1,0:T(8,128)(2,1)S(1)}, bf16[368,128]{1,0:T(8,128)(2,1)S(1)}, u32[]{:S(2)}, u32[]{:S(2)}) collective-permute-start(bf16[368,128]{1,0:T(8,128)(2,1)S(1)} %get-tuple-element.38), channel_id=1, source_target_pairs={{1,2},{3,0},{2,1},{0,3},{5,6},{7,4},{6,5},{4,7},{9,10},{11,8},{10,... | collective-permute-start | bytes 282632 | tf_op jit(solution)/shard_map/ppermute | solution.py:558
  15.4 1.2 %collective-permute-start.3 = (bf16[368,128]{1,0:T(8,128)(2,1)S(1)}, bf16[368,128]{1,0:T(8,128)(2,1)S(1)}, u32[]{:S(2)}, u32[]{:S(2)}) collective-permute-start(bf16[368,128]{1,0:T(8,128)(2,1)S(1)} %get-tuple-element.39), channel_id=1, source_target_pairs={{0,1},{2,3},{1,0},{3,2},{4,5},{6,7},{5,4},{7,6},{8,9},{10,11},{9,8... | collective-permute-start | bytes 282632 | tf_op jit(solution)/shard_map/ppermute | solution.py:558
  16.6 0.1 collective-permute-start.4
  16.8 0.5 %collective-permute-start.5 = (bf16[256,128]{1,0:T(8,128)(2,1)S(1)}, bf16[256,128]{1,0:T(8,128)(2,1)S(1)}, u32[]{:S(2)}, u32[]{:S(2)}) collective-permute-start(bf16[256,128]{1,0:T(8,128)(2,1)S(1)} %get-tuple-element.42), channel_id=1, source_target_pairs={{0,1},{2,3},{1,0},{3,2},{4,5},{6,7},{5,4},{7,6},{8,9},{10,11},{9,8... | collective-permute-start | bytes 196616 | tf_op jit(solution)/shard_map/ppermute | solution.py:558
  17.3 2.1 %by_operator.3.second_ref = bf16[320,32,128]{2,1,0:T(8,128)(2,1)S(1)} custom-call(bf16[121,316,121]{2,1,0:T(8,128)(2,1)} %bitcast.22), custom_call_target="tpu_custom_call" | custom-call | bytes 5242880 | tf_op jit(solution)/shard_map/by_operator/pallas_call | solution.py:74
  19.4 0.1 inner_pairs.1
  19.5 0.5 %collective-permute-done.2.y_odd = bf16[368,128]{1,0:T(8,128)(2,1)S(1)} collective-permute-done((bf16[368,128]{1,0:T(8,128)(2,1)S(1)}, bf16[368,128]{1,0:T(8,128)(2,1)S(1)}, u32[]{:S(2)}, u32[]{:S(2)}) %collective-permute-start.2) | collective-permute-done | bytes 94240 | tf_op jit(solution)/shard_map/ppermute | solution.py:558
  20.0 0.0 collective-permute-done.3.y_even
  20.0 0.0 copy-start
  20.0 2.9 %m2l.1.local_ref = bf16[128,128]{1,0:T(8,128)(2,1)S(1)} custom-call(bf16[350,16,128]{2,1,0:T(8,128)(2,1)S(1)} %get-tuple-element.34.inner, f32[10,7,8,128]{3,2,1,0:T(8,128)S(1)} %get-tuple-element.35.along_x, bf16[368,128]{1,0:T(8,128)(2,1)S(1)} %collective-permute-done.2.y_odd, bf16[368,128]{1,0:T(8,128)(2,1)S(1)} %collective-permute-done.3.y_even, ...), custom_call_target="tpu_custom_call" | custom-call | bytes 65536 | tf_op jit(solution)/shard_map/m2l/pallas_call | solution.py:390
  22.9 0.0 collective-permute-done.4.odd_passed
  22.9 0.0 collective-permute-done.5.even_passed
  22.9 0.3 answer.1
  23.2 0.3 collective-permute-start.6
  23.4 1.4 %collective-permute-start.7 = (f32[8,128]{1,0:T(8,128)S(1)}, f32[8,128]{1,0:T(8,128)S(1)}, u32[]{:S(2)}, u32[]{:S(2)}) collective-permute-start(f32[8,128]{1,0:T(8,128)S(1)} %get-tuple-element.45.up_ref), channel_id=1, source_target_pairs={{1,2},{3,0},{2,1},{0,3},{5,6},{7,4},{6,5},{4,7},{9,10},{11,8},{10,... | collective-permute-start | bytes 12296 | tf_op jit(solution)/shard_map/ppermute | solution.py:558
  24.8 0.0 collective-permute-done.6.y_even
  24.8 1.6 %collective-permute-done.7.y_odd = f32[8,128]{1,0:T(8,128)S(1)} collective-permute-done((f32[8,128]{1,0:T(8,128)S(1)}, f32[8,128]{1,0:T(8,128)S(1)}, u32[]{:S(2)}, u32[]{:S(2)}) %collective-permute-start.7) | collective-permute-done | bytes 4128 | tf_op jit(solution)/shard_map/ppermute | solution.py:558
  26.5 2.9 %collective-permute-start.8 = (f32[8,128]{1,0:T(8,128)S(1)}, f32[8,128]{1,0:T(8,128)S(1)}, u32[]{:S(2)}, u32[]{:S(2)}) collective-permute-start(f32[8,128]{1,0:T(8,128)S(1)} %get-tuple-element.50), channel_id=1, source_target_pairs={{4,8},{12,16},{20,24},{28,0},{8,4},{16,12},{24,20},{0,28},{5,9},{1... | collective-permute-start | bytes 12296 | tf_op jit(solution)/shard_map/ppermute | solution.py:558
  29.4 0.0 collective-permute-start.9
  29.4 0.0 copy-done
  29.4 0.0 copy-done.1
  29.4 0.0 copy-done.2
  29.4 2.7 %atoms.1 = (bf16[121,128]{1,0:T(8,128)(2,1)}, f32[4,2048]{1,0:T(4,128)S(1)}, f32[9,128]{1,0:T(8,128)}) custom-call(s32[16,128]{1,0:T(8,128)S(1)} %bitcast.18, s32[16,128]{1,0:T(8,128)S(1)} %bitcast.20, bf16[64,128]{1,0:T(8,128)(2,1)S(1)} %bitcast.16, bf16[4,128,2048]{2,1,0:T(8,128)(2,1)S(1)} %get-tuple-element.28.rows_ref, ...), custom_call_target="tpu_custom_call" | custom-call | flops 4000000 | bytes 8388608 | tf_op jit(solution)/shard_map/atoms/pallas_call | solution.py:483
  32.1 0.7 %collective-permute-done.8.x_odd = f32[8,128]{1,0:T(8,128)S(1)} collective-permute-done((f32[8,128]{1,0:T(8,128)S(1)}, f32[8,128]{1,0:T(8,128)S(1)}, u32[]{:S(2)}, u32[]{:S(2)}) %collective-permute-start.8) | collective-permute-done | bytes 4128 | tf_op jit(solution)/shard_map/ppermute | solution.py:558
  32.8 0.2 collective-permute-done.9.x_even
  33.0 1.0 %merge.1 = f32[4,2048]{1,0:T(4,128)} custom-call(f32[4,2048]{1,0:T(4,128)S(1)} %get-tuple-element.48.far_ref, bf16[256,2048]{1,0:T(8,128)(2,1)S(1)} %get-tuple-element.49.place_ref, f32[8,128]{1,0:T(8,128)S(1)} %collective-permute-done.8.x_odd, f32[8,128]{1,0:T(8,128)S(1)} %collective-permute-done.9.x_even, f32[8,128]{1,0:T(8,128)S(1)} %collective-permute-done.7.y_odd, ...), custom_call_target="tpu_custom_call" | custom-call | tf_op jit(solution)/shard_map/merge/pallas_call | solution.py:545
  (4 shorter events, 0.0 us)
Async XLA Ops:
  3.7 11.2 %collective-permute-start = (bf16[480,128]{1,0:T(8,128)(2,1)S(1)}, bf16[480,128]{1,0:T(8,128)(2,1)S(1)}, u32[]{:S(2)}, u32[]{:S(2)}) collective-permute-start(bf16[480,128]{1,0:T(8,128)(2,1)S(1)} %get-tuple-element.30), channel_id=1, source_target_pairs={{0,4},{8,12},{16,20},{24,28},{4,0},{12,8},{20,16},{28,24},{1,5},{9... | collective-permute-start | bytes 368648 | tf_op jit(solution)/shard_map/ppermute | solution.py:558
  6.7 8.2 %collective-permute-start.1 = (bf16[480,128]{1,0:T(8,128)(2,1)S(1)}, bf16[480,128]{1,0:T(8,128)(2,1)S(1)}, u32[]{:S(2)}, u32[]{:S(2)}) collective-permute-start(bf16[480,128]{1,0:T(8,128)(2,1)S(1)} %get-tuple-element.31), channel_id=1, source_target_pairs={{4,8},{12,16},{20,24},{28,0},{8,4},{16,12},{24,20},{0,28},{5,9},{1... | collective-permute-start | bytes 368648 | tf_op jit(solution)/shard_map/ppermute | solution.py:558
  15.0 5.0 %collective-permute-start.2 = (bf16[368,128]{1,0:T(8,128)(2,1)S(1)}, bf16[368,128]{1,0:T(8,128)(2,1)S(1)}, u32[]{:S(2)}, u32[]{:S(2)}) collective-permute-start(bf16[368,128]{1,0:T(8,128)(2,1)S(1)} %get-tuple-element.38), channel_id=1, source_target_pairs={{1,2},{3,0},{2,1},{0,3},{5,6},{7,4},{6,5},{4,7},{9,10},{11,8},{10,... | collective-permute-start | bytes 282632 | tf_op jit(solution)/shard_map/ppermute | solution.py:558
  15.4 4.6 %collective-permute-start.3 = (bf16[368,128]{1,0:T(8,128)(2,1)S(1)}, bf16[368,128]{1,0:T(8,128)(2,1)S(1)}, u32[]{:S(2)}, u32[]{:S(2)}) collective-permute-start(bf16[368,128]{1,0:T(8,128)(2,1)S(1)} %get-tuple-element.39), channel_id=1, source_target_pairs={{0,1},{2,3},{1,0},{3,2},{4,5},{6,7},{5,4},{7,6},{8,9},{10,11},{9,8... | collective-permute-start | bytes 282632 | tf_op jit(solution)/shard_map/ppermute | solution.py:558
  16.6 6.3 %collective-permute-start.4 = (bf16[256,128]{1,0:T(8,128)(2,1)S(1)}, bf16[256,128]{1,0:T(8,128)(2,1)S(1)}, u32[]{:S(2)}, u32[]{:S(2)}) collective-permute-start(bf16[256,128]{1,0:T(8,128)(2,1)S(1)} %get-tuple-element.41), channel_id=1, source_target_pairs={{1,2},{3,0},{2,1},{0,3},{5,6},{7,4},{6,5},{4,7},{9,10},{11,8},{10,... | collective-permute-start | bytes 196616 | tf_op jit(solution)/shard_map/ppermute | solution.py:558
  16.8 6.1 %collective-permute-start.5 = (bf16[256,128]{1,0:T(8,128)(2,1)S(1)}, bf16[256,128]{1,0:T(8,128)(2,1)S(1)}, u32[]{:S(2)}, u32[]{:S(2)}) collective-permute-start(bf16[256,128]{1,0:T(8,128)(2,1)S(1)} %get-tuple-element.42), channel_id=1, source_target_pairs={{0,1},{2,3},{1,0},{3,2},{4,5},{6,7},{5,4},{7,6},{8,9},{10,11},{9,8... | collective-permute-start | bytes 196616 | tf_op jit(solution)/shard_map/ppermute | solution.py:558
  20.0 9.4 %copy-start = (bf16[4,2048]{1,0:T(4,128)(2,1)S(1)}, bf16[4,2048]{1,0:T(4,128)(2,1)}, u32[]{:S(2)}) copy-start(bf16[4,2048]{1,0:T(4,128)(2,1)} %param.11) | copy-start | bytes 49156
  20.0 9.4 %copy-start.1 = (s32[2048,1]{0,1:T(1,128)S(1)}, s32[2048,1]{0,1:T(1,128)}, u32[]{:S(2)}) copy-start(s32[2048,1]{0,1:T(1,128)} %param.12) | copy-start | bytes 24580
  20.0 9.4 %copy-start.2 = (s32[2048]{0:T(1024)S(1)}, s32[2048]{0:T(1024)}, u32[]{:S(2)}) copy-start(s32[2048]{0:T(1024)} %param.13) | copy-start | bytes 24580
  23.2 1.7 %collective-permute-start.6 = (f32[8,128]{1,0:T(8,128)S(1)}, f32[8,128]{1,0:T(8,128)S(1)}, u32[]{:S(2)}, u32[]{:S(2)}) collective-permute-start(f32[8,128]{1,0:T(8,128)S(1)} %get-tuple-element.44.down_ref), channel_id=1, source_target_pairs={{0,1},{2,3},{1,0},{3,2},{4,5},{6,7},{5,4},{7,6},{8,9},{10,11},{9,8... | collective-permute-start | bytes 12296 | tf_op jit(solution)/shard_map/ppermute | solution.py:558
  23.4 3.0 %collective-permute-start.7 = (f32[8,128]{1,0:T(8,128)S(1)}, f32[8,128]{1,0:T(8,128)S(1)}, u32[]{:S(2)}, u32[]{:S(2)}) collective-permute-start(f32[8,128]{1,0:T(8,128)S(1)} %get-tuple-element.45.up_ref), channel_id=1, source_target_pairs={{1,2},{3,0},{2,1},{0,3},{5,6},{7,4},{6,5},{4,7},{9,10},{11,8},{10,... | collective-permute-start | bytes 12296 | tf_op jit(solution)/shard_map/ppermute | solution.py:558
  26.5 6.3 %collective-permute-start.8 = (f32[8,128]{1,0:T(8,128)S(1)}, f32[8,128]{1,0:T(8,128)S(1)}, u32[]{:S(2)}, u32[]{:S(2)}) collective-permute-start(f32[8,128]{1,0:T(8,128)S(1)} %get-tuple-element.50), channel_id=1, source_target_pairs={{4,8},{12,16},{20,24},{28,0},{8,4},{16,12},{24,20},{0,28},{5,9},{1... | collective-permute-start | bytes 12296 | tf_op jit(solution)/shard_map/ppermute | solution.py:558
  29.4 3.6 %collective-permute-start.9 = (f32[8,128]{1,0:T(8,128)S(1)}, f32[8,128]{1,0:T(8,128)S(1)}, u32[]{:S(2)}, u32[]{:S(2)}) collective-permute-start(f32[8,128]{1,0:T(8,128)S(1)} %get-tuple-element.51), channel_id=1, source_target_pairs={{0,4},{8,12},{16,20},{24,28},{4,0},{12,8},{20,16},{28,24},{1,5},{9... | collective-permute-start | bytes 12296 | tf_op jit(solution)/shard_map/ppermute | solution.py:558

commit v2 on v1

--- a/solution.py
+++ b/solution.py
@@ -19,9 +19,9 @@
 SLAB_X = REACH * BY * BZ
 SLAB_Y = BX * REACH * BZ + 2 * REACH * REACH * BZ
 FIELDS = 4
-STEP = 40
+STEP = 316
 AROUND = [(1, 1), (1, 0), (1, 2), (2, 1), (2, 0), (2, 2), (0, 1), (0, 2)]
-SENDERS = [(0, 1), (1, 1), (2, 1), (0, 2), (1, 2), (2, 2), (1, 0), (2, 0)]
+SENDERS = [(1, 0), (1, 1), (1, 2), (2, 0), (2, 1), (2, 2), (0, 1), (0, 2)]
 
 
 def offsets():
@@ -63,9 +63,8 @@
                 x = jnp.concatenate([x.astype(F32), jnp.zeros((some, k0 + 16 - noff, terms), F32)], axis=1).astype(BF)
             if some < 16:
                 x = jnp.concatenate([x, jnp.zeros((16 - some, 16, terms), BF)], axis=0)
-            x = jnp.swapaxes(x, 0, 1)
             x = jnp.concatenate([x, jnp.zeros((16, 16, LANES - terms), BF)], axis=2)
-            out_ref[k0 : k0 + 16, rows, :] = x
+            out_ref[k0 : k0 + 16, rows, :] = jnp.swapaxes(x, 0, 1)
 
 
 def by_operator(ops, first, steps):
@@ -361,10 +360,11 @@
 
 
 def messages(x_even, x_odd, y_even, y_odd, even_passed, odd_passed):
-    along_y = []
-    for direct, passed in ((y_even, even_passed), (y_odd, odd_passed)):
-        along_y += [(direct, SLAB_Y), (passed, 0), (passed, LANES)]
-    return along_y + [(x_even, SLAB_X + LANES), (x_odd, SLAB_X + LANES)]
+    direct = SLAB_X + LANES
+    return [
+        (x_even, direct), (even_passed, 0), (odd_passed, 0), (x_odd, direct), (even_passed, LANES), (odd_passed, LANES),
+        (y_even, SLAB_Y), (y_odd, SLAB_Y),
+    ]
 
 
 def m2l_kernel(inner, along_x, y_odd, y_even, first_ref, second_ref, local_ref, grid, outer):
@@ -402,7 +402,7 @@
     )(pinned[0], pinned[1], y_odd, y_even, pinned[2], pinned[3])
 
 
-def answer_kernel(terms, local_ref, x_odd, x_even, y_odd, y_even, odd_passed, even_passed, down_ref, up_ref, side_ref, tail_ref):
+def answer_kernel(terms, local_ref, x_odd, x_even, y_odd, y_even, odd_passed, even_passed, by_even_ref, by_odd_ref, by_y_ref, tail_ref):
     local = local_ref[...]
     row = lax.broadcasted_iota(jnp.int32, (8, LANES), 0)
     answers = []
@@ -413,7 +413,7 @@
         spread = one_hot(x[terms + 1 : terms + 2].astype(jnp.int32), LANES)
         column = jnp.dot(local, spread, preferred_element_type=F32)
         answers.append(jnp.sum(x[:terms] * column[:terms], axis=0, keepdims=True))
-    for ref, first in ((down_ref, 0), (up_ref, 3), (side_ref, 6)):
+    for ref, first in ((by_even_ref, 0), (by_odd_ref, 3), (by_y_ref, 6)):
         tile = jnp.zeros((8, LANES), F32)
         for i in range(min(3, 8 - first)):
             tile = jnp.where(row == i, answers[first + i], tile)
@@ -433,7 +433,7 @@
 
 
 def atoms_kernel(size_y, owner_ref, slot_ref, ion_ref, rows_ref, local_ref, tail_ref,
-                 down_ref, up_ref, side_ref, local_exp_ref, far_ref, virial_ref):
+                 by_even_ref, by_odd_ref, by_y_ref, local_exp_ref, far_ref, virial_ref):
     chunks = slot_ref.shape[0]
     local = local_ref[...]
     local_exp_ref[...] = local[: local_exp_ref.shape[0]]
@@ -453,9 +453,9 @@
         terms3 = jnp.concatenate([ion[0:1] * ion[a : a + 1] * far for a in (1, 2, 3)], axis=0)
         total = total + nt(split3(terms3), spread)
 
-    per_peer = side_ref.shape[1] // FIELDS
+    per_peer = by_y_ref.shape[1] // FIELDS
     group = lax.broadcasted_iota(jnp.int32, (8, LANES), 1) // per_peer
-    answers = [(down_ref, 0), (down_ref, 1), (down_ref, 2), (up_ref, 0), (up_ref, 1), (up_ref, 2), (side_ref, 0), (side_ref, 1)]
+    answers = [(ref, i) for ref in (by_even_ref, by_odd_ref) for i in range(3)] + [(by_y_ref, 0), (by_y_ref, 1)]
     for n, (answer, i) in enumerate(answers):
         d = AROUND.index(SENDERS[n])
         spread = one_hot(tail_ref[8 + n : 9 + n].astype(jnp.int32), LANES)
@@ -492,12 +492,12 @@
     )(owner.reshape(chunks, LANES), slot.reshape(chunks, LANES), ions, pltpu.with_memory_space_constraint(rows, pltpu.VMEM), local, tail, down, up_, side)
 
 
-def turn_kernel(answer_x, y_even, y_odd, x_odd_ref, x_even_ref):
-    for n, ref in ((1, x_even_ref), (2, x_odd_ref)):
+def turn_kernel(answer_y, x_even, x_odd, y_odd_ref, y_even_ref):
+    for n, ref in ((1, y_even_ref), (2, y_odd_ref)):
         ref[...] = jnp.zeros(ref.shape, F32)
-        ref[0:1] = answer_x[n - 1 : n]
-        ref[1:2] = y_odd[n : n + 1]
-        ref[2:3] = y_even[n : n + 1]
+        ref[0:1] = answer_y[n - 1 : n]
+        ref[1:2] = x_even[n : n + 1]
+        ref[2:3] = x_odd[n : n + 1]
 
 
 def turn(*operands):
@@ -516,9 +516,9 @@
     per_peer = place_ref.shape[0] // 8
     each = LANES // per_peer
     returned = {
-        (0, 1): (y_even, 0), (0, 2): (y_odd, 0),
-        (1, 0): (x_even, 0), (1, 2): (x_even, 1), (1, 1): (x_even, 2),
-        (2, 0): (x_odd, 0), (2, 2): (x_odd, 1), (2, 1): (x_odd, 2),
+        (1, 0): (x_even, 0), (2, 0): (x_odd, 0),
+        (0, 1): (y_even, 0), (1, 1): (y_even, 1), (2, 1): (y_even, 2),
+        (0, 2): (y_odd, 0), (1, 2): (y_odd, 1), (2, 2): (y_odd, 2),
     }
     row = lax.broadcasted_iota(jnp.int32, (8, LANES), 0)
     group = lax.broadcasted_iota(jnp.int32, (8, LANES), 1) // per_peer
@@ -585,18 +585,19 @@
     second = by_operator(translation_ops, 6, 2)
     inner, along_x = inner_pairs(own, x_even, x_odd)
     local = m2l(inner, along_x, y_odd, y_even, first, second)
-    answer_y_even, answer_y_odd, answer_x, tail = answer(
+    answer_x_even, answer_x_odd, answer_y, tail = answer(
         num_terms, local, x_odd, x_even, y_odd, y_even, odd_messages, even_messages
     )
 
+    back_x_even = across("xs", 1, answer_x_even)
+    back_x_odd = across("xs", 2, answer_x_odd)
+    local_exp, far, box_virial = atoms_of_device(
+        num_terms, size_y, atom_owner, atom_slot, ion_data, rows, local, tail, answer_x_even, answer_x_odd, answer_y
+    )
+    back_x_even, back_x_odd, far = lax.optimization_barrier((back_x_even, back_x_odd, far))
+    answer_y_odd, answer_y_even = turn(answer_y, back_x_even, back_x_odd)
     back_y_odd = across("ys", 2, answer_y_odd)
     back_y_even = across("ys", 1, answer_y_even)
-    local_exp, far, box_virial = atoms_of_device(
-        num_terms, size_y, atom_owner, atom_slot, ion_data, rows, local, tail, answer_y_even, answer_y_odd, answer_x
-    )
-    answer_x_odd, answer_x_even = turn(answer_x, back_y_even, back_y_odd)
-    back_x_odd = across("xs", 2, answer_x_odd)
-    back_x_even = across("xs", 1, answer_x_even)
     atom_far_field = merge(far, place, back_x_odd, back_x_even, back_y_odd, back_y_even)
     return (local_exp, atom_far_field, box_virial)
 

time: 34.1 us -> 33.3 us (0.977)
  waiting for transfers between devices: 2.99 us -> 2.2 us
  starting transfers between devices: 13.5 us -> 14.1 us
  Pallas kernels: 16.7 us -> 16.1 us
    ppermute x10, waiting for transfers between devices: 2.99 us -> 2.2 us  [across(): return lax.ppermute(block, axis, pairs + [(b, a) for a, b in pairs])]
    pallas_call x2, Pallas kernels: 6.72 us -> 6.06 us  [by_operator(): pl.pallas_call(functools.partial(by_operator_kernel, first), in_specs=[pl...]
    ppermute x10, starting transfers between devices: 13.5 us -> 14.1 us  [across(): return lax.ppermute(block, axis, pairs + [(b, a) for a, b in pairs])]
  transfers between devices with their start and end apart: 10 -> 10, of which waited for: 4 -> 3; matrix products, arithmetic and copies ran while one was open for 0% -> 0% of each run, Pallas kernels for 37% -> 36%
where the time goes in v2:
time: 33.3 us; the launch traced here: 33.1 us
  Pallas kernels  16.1 us (48%)
  starting transfers between devices  14.1 us (42%)
  waiting for transfers between devices  2.2 us (7%)
  between operations  0.74 us (2%)
    ppermute x10, starting transfers between devices, across(): return lax.ppermute(block, axis, pairs + [(b, a) for a, b in pairs])  14.1 us
    pallas_call x2, Pallas kernels, by_operator(): pl.pallas_call(functools.partial(by_operator_kernel, first), in_specs=[pl...  6.06 us
    pallas_call x1, Pallas kernels, pack(): pl.pallas_call(functools.partial(pack_kernel, sizes), in_specs=[pl.BlockS...  3.05 us
    pallas_call x1, Pallas kernels, m2l(): pl.pallas_call(m2l_kernel, in_specs=[vmem] * 6, out_specs=vmem, out_shape...  2.87 us
    pallas_call x1, Pallas kernels, atoms_of_device(): pl.pallas_call(functools.partial(atoms_kernel, size_y), in_specs=[whole]...  2.72 us
    ppermute x10, waiting for transfers between devices, across(): return lax.ppermute(block, axis, pairs + [(b, a) for a, b in pairs])  2.2 us
    pallas_call x1, Pallas kernels, merge(): pl.pallas_call(merge_kernel, in_specs=[whole] * 6, out_specs=whole, out_s...  0.96 us
  transfers between devices with their start and end apart: 10, of which 3 were waited for; matrix products, arithmetic and copies ran while one was open for 0% of the time, Pallas kernels for 36%

profile of v2, /device:TPU:0, one launch (start us, length us, event | category | flops | bytes accessed | tf_op | source)
XLA Modules:
  0.0 33.1 jit_solution(7264796228326880741)
XLA Ops:
  0.6 3.1 %pack.1 = (bf16[128,128]{1,0:T(8,128)(2,1)S(1)}, bf16[480,128]{1,0:T(8,128)(2,1)S(1)}, bf16[480,128]{1,0:T(8,128)(2,1)S(1)}, bf16[128,128]{1,0:T(8,128)(2,1)S(1)...) custom-call(s32[16,128]{1,0:T(8,128)} %bitcast.17, ...), custom_call_target="tpu_custom_call" | custom-call | tf_op jit(solution)/shard_map/pack/pallas_call | solution.py:255
  3.7 3.0 %collective-permute-start = (bf16[480,128]{1,0:T(8,128)(2,1)S(1)}, bf16[480,128]{1,0:T(8,128)(2,1)S(1)}, u32[]{:S(2)}, u32[]{:S(2)}) collective-permute-start(bf16[480,128]{1,0:T(8,128)(2,1)S(1)} %get-tuple-element.33), channel_id=1, source_target_pairs={{0,4},{8,12},{16,20},{24,28},{4,0},{12,8},{20,16},{28,24},{1,5},{9... | collective-permute-start | bytes 368648 | tf_op jit(solution)/shard_map/ppermute | solution.py:558
  6.7 3.5 %collective-permute-start.1 = (bf16[480,128]{1,0:T(8,128)(2,1)S(1)}, bf16[480,128]{1,0:T(8,128)(2,1)S(1)}, u32[]{:S(2)}, u32[]{:S(2)}) collective-permute-start(bf16[480,128]{1,0:T(8,128)(2,1)S(1)} %get-tuple-element.34), channel_id=1, source_target_pairs={{4,8},{12,16},{20,24},{28,0},{8,4},{16,12},{24,20},{0,28},{5,9},{1... | collective-permute-start | bytes 368648 | tf_op jit(solution)/shard_map/ppermute | solution.py:558
  10.3 4.1 %by_operator.2.first_ref = bf16[320,96,128]{2,1,0:T(8,128)(2,1)S(1)} custom-call(bf16[121,316,121]{2,1,0:T(8,128)(2,1)} %bitcast.21), custom_call_target="tpu_custom_call" | custom-call | bytes 15728640 | tf_op jit(solution)/shard_map/by_operator/pallas_call | solution.py:73
  14.4 0.0 collective-permute-done.x_even
  14.4 0.0 collective-permute-done.1.x_odd
  14.4 0.4 %collective-permute-start.2 = (bf16[368,128]{1,0:T(8,128)(2,1)S(1)}, bf16[368,128]{1,0:T(8,128)(2,1)S(1)}, u32[]{:S(2)}, u32[]{:S(2)}) collective-permute-start(bf16[368,128]{1,0:T(8,128)(2,1)S(1)} %get-tuple-element.41), channel_id=1, source_target_pairs={{1,2},{3,0},{2,1},{0,3},{5,6},{7,4},{6,5},{4,7},{9,10},{11,8},{10,... | collective-permute-start | bytes 282632 | tf_op jit(solution)/shard_map/ppermute | solution.py:558
  14.9 1.2 %collective-permute-start.3 = (bf16[368,128]{1,0:T(8,128)(2,1)S(1)}, bf16[368,128]{1,0:T(8,128)(2,1)S(1)}, u32[]{:S(2)}, u32[]{:S(2)}) collective-permute-start(bf16[368,128]{1,0:T(8,128)(2,1)S(1)} %get-tuple-element.42), channel_id=1, source_target_pairs={{0,1},{2,3},{1,0},{3,2},{4,5},{6,7},{5,4},{7,6},{8,9},{10,11},{9,8... | collective-permute-start | bytes 282632 | tf_op jit(solution)/shard_map/ppermute | solution.py:558
  16.1 0.1 collective-permute-start.4
  16.3 0.5 %collective-permute-start.5 = (bf16[256,128]{1,0:T(8,128)(2,1)S(1)}, bf16[256,128]{1,0:T(8,128)(2,1)S(1)}, u32[]{:S(2)}, u32[]{:S(2)}) collective-permute-start(bf16[256,128]{1,0:T(8,128)(2,1)S(1)} %get-tuple-element.45), channel_id=1, source_target_pairs={{0,1},{2,3},{1,0},{3,2},{4,5},{6,7},{5,4},{7,6},{8,9},{10,11},{9,8... | collective-permute-start | bytes 196616 | tf_op jit(solution)/shard_map/ppermute | solution.py:558
  16.8 1.9 %by_operator.3.second_ref = bf16[320,32,128]{2,1,0:T(8,128)(2,1)S(1)} custom-call(bf16[121,316,121]{2,1,0:T(8,128)(2,1)} %bitcast.22), custom_call_target="tpu_custom_call" | custom-call | bytes 5242880 | tf_op jit(solution)/shard_map/by_operator/pallas_call | solution.py:73
  18.7 0.1 inner_pairs.1
  18.9 0.6 %collective-permute-done.2.y_odd = bf16[368,128]{1,0:T(8,128)(2,1)S(1)} collective-permute-done((bf16[368,128]{1,0:T(8,128)(2,1)S(1)}, bf16[368,128]{1,0:T(8,128)(2,1)S(1)}, u32[]{:S(2)}, u32[]{:S(2)}) %collective-permute-start.2) | collective-permute-done | bytes 94240 | tf_op jit(solution)/shard_map/ppermute | solution.py:558
  19.5 0.0 collective-permute-done.3.y_even
  19.5 0.0 copy-start
  19.5 2.9 %m2l.1.local_ref = bf16[128,128]{1,0:T(8,128)(2,1)S(1)} custom-call(bf16[350,16,128]{2,1,0:T(8,128)(2,1)S(1)} %get-tuple-element.37.inner, f32[10,7,8,128]{3,2,1,0:T(8,128)S(1)} %get-tuple-element.38.along_x, bf16[368,128]{1,0:T(8,128)(2,1)S(1)} %collective-permute-done.2.y_odd, bf16[368,128]{1,0:T(8,128)(2,1)S(1)} %collective-permute-done.3.y_even, ...), custom_call_target="tpu_custom_call" | custom-call | bytes 65536 | tf_op jit(solution)/shard_map/m2l/pallas_call | solution.py:390
  22.4 0.0 collective-permute-done.4.odd_passed
  22.4 0.0 collective-permute-done.5.even_passed
  22.4 0.2 answer.1
  22.6 0.1 collective-permute-start.6
  22.7 3.5 %collective-permute-start.7 = (f32[8,128]{1,0:T(8,128)S(1)}, f32[8,128]{1,0:T(8,128)S(1)}, u32[]{:S(2)}, u32[]{:S(2)}) collective-permute-start(f32[8,128]{1,0:T(8,128)S(1)} %get-tuple-element.48.by_odd_ref), channel_id=1, source_target_pairs={{4,8},{12,16},{20,24},{28,0},{8,4},{16,12},{24,20},{0,28},{5,9},{1... | collective-permute-start | bytes 12296 | tf_op jit(solution)/shard_map/ppermute | solution.py:558
  26.3 0.0 copy-done
  26.3 0.0 copy-done.1
  26.3 0.0 copy-done.2
  26.3 2.7 %atoms.1 = (bf16[121,128]{1,0:T(8,128)(2,1)}, f32[4,2048]{1,0:T(4,128)S(1)}, f32[9,128]{1,0:T(8,128)}) custom-call(s32[16,128]{1,0:T(8,128)S(1)} %bitcast.18, s32[16,128]{1,0:T(8,128)S(1)} %bitcast.20, bf16[64,128]{1,0:T(8,128)(2,1)S(1)} %bitcast.16, bf16[4,128,2048]{2,1,0:T(8,128)(2,1)S(1)} %get-tuple-element.31.rows_ref, ...), custom_call_target="tpu_custom_call" | custom-call | flops 4000000 | bytes 8388608 | tf_op jit(solution)/shard_map/atoms/pallas_call | solution.py:483
  29.0 0.0 collective-permute-done.6.x_even
  29.0 0.1 collective-permute-done.7.x_odd
  29.1 0.2 collective-permute-start.8
  29.3 1.4 %collective-permute-start.9 = (f32[8,128]{1,0:T(8,128)S(1)}, f32[8,128]{1,0:T(8,128)S(1)}, u32[]{:S(2)}, u32[]{:S(2)}) collective-permute-start(f32[8,128]{1,0:T(8,128)S(1)} %get-tuple-element.57), channel_id=1, source_target_pairs={{0,1},{2,3},{1,0},{3,2},{4,5},{6,7},{5,4},{7,6},{8,9},{10,11},{9,8... | collective-permute-start | bytes 12296 | tf_op jit(solution)/shard_map/ppermute | solution.py:558
  30.7 1.5 %collective-permute-done.8.y_odd = f32[8,128]{1,0:T(8,128)S(1)} collective-permute-done((f32[8,128]{1,0:T(8,128)S(1)}, f32[8,128]{1,0:T(8,128)S(1)}, u32[]{:S(2)}, u32[]{:S(2)}) %collective-permute-start.8) | collective-permute-done | bytes 4128 | tf_op jit(solution)/shard_map/ppermute | solution.py:558
  32.1 0.0 collective-permute-done.9.y_even
  32.1 1.0 %merge.1 = f32[4,2048]{1,0:T(4,128)} custom-call(f32[4,2048]{1,0:T(4,128)S(1)} %get-tuple-element.52.far_ref, bf16[256,2048]{1,0:T(8,128)(2,1)S(1)} %get-tuple-element.53.place_ref, f32[8,128]{1,0:T(8,128)S(1)} %collective-permute-done.7.x_odd, f32[8,128]{1,0:T(8,128)S(1)} %collective-permute-done.6.x_even, f32[8,128]{1,0:T(8,128)S(1)} %collective-permute-done.8.y_odd, ...), custom_call_target="tpu_custom_call" | custom-call | tf_op jit(solution)/shard_map/merge/pallas_call | solution.py:545
  (4 shorter events, 0.0 us)
Async XLA Ops:
  3.7 10.7 %collective-permute-start = (bf16[480,128]{1,0:T(8,128)(2,1)S(1)}, bf16[480,128]{1,0:T(8,128)(2,1)S(1)}, u32[]{:S(2)}, u32[]{:S(2)}) collective-permute-start(bf16[480,128]{1,0:T(8,128)(2,1)S(1)} %get-tuple-element.33), channel_id=1, source_target_pairs={{0,4},{8,12},{16,20},{24,28},{4,0},{12,8},{20,16},{28,24},{1,5},{9... | collective-permute-start | bytes 368648 | tf_op jit(solution)/shard_map/ppermute | solution.py:558
  6.7 7.7 %collective-permute-start.1 = (bf16[480,128]{1,0:T(8,128)(2,1)S(1)}, bf16[480,128]{1,0:T(8,128)(2,1)S(1)}, u32[]{:S(2)}, u32[]{:S(2)}) collective-permute-start(bf16[480,128]{1,0:T(8,128)(2,1)S(1)} %get-tuple-element.34), channel_id=1, source_target_pairs={{4,8},{12,16},{20,24},{28,0},{8,4},{16,12},{24,20},{0,28},{5,9},{1... | collective-permute-start | bytes 368648 | tf_op jit(solution)/shard_map/ppermute | solution.py:558
  14.4 5.0 %collective-permute-start.2 = (bf16[368,128]{1,0:T(8,128)(2,1)S(1)}, bf16[368,128]{1,0:T(8,128)(2,1)S(1)}, u32[]{:S(2)}, u32[]{:S(2)}) collective-permute-start(bf16[368,128]{1,0:T(8,128)(2,1)S(1)} %get-tuple-element.41), channel_id=1, source_target_pairs={{1,2},{3,0},{2,1},{0,3},{5,6},{7,4},{6,5},{4,7},{9,10},{11,8},{10,... | collective-permute-start | bytes 282632 | tf_op jit(solution)/shard_map/ppermute | solution.py:558
  14.9 4.6 %collective-permute-start.3 = (bf16[368,128]{1,0:T(8,128)(2,1)S(1)}, bf16[368,128]{1,0:T(8,128)(2,1)S(1)}, u32[]{:S(2)}, u32[]{:S(2)}) collective-permute-start(bf16[368,128]{1,0:T(8,128)(2,1)S(1)} %get-tuple-element.42), channel_id=1, source_target_pairs={{0,1},{2,3},{1,0},{3,2},{4,5},{6,7},{5,4},{7,6},{8,9},{10,11},{9,8... | collective-permute-start | bytes 282632 | tf_op jit(solution)/shard_map/ppermute | solution.py:558
  16.1 6.2 %collective-permute-start.4 = (bf16[256,128]{1,0:T(8,128)(2,1)S(1)}, bf16[256,128]{1,0:T(8,128)(2,1)S(1)}, u32[]{:S(2)}, u32[]{:S(2)}) collective-permute-start(bf16[256,128]{1,0:T(8,128)(2,1)S(1)} %get-tuple-element.44), channel_id=1, source_target_pairs={{1,2},{3,0},{2,1},{0,3},{5,6},{7,4},{6,5},{4,7},{9,10},{11,8},{10,... | collective-permute-start | bytes 196616 | tf_op jit(solution)/shard_map/ppermute | solution.py:558
  16.3 6.1 %collective-permute-start.5 = (bf16[256,128]{1,0:T(8,128)(2,1)S(1)}, bf16[256,128]{1,0:T(8,128)(2,1)S(1)}, u32[]{:S(2)}, u32[]{:S(2)}) collective-permute-start(bf16[256,128]{1,0:T(8,128)(2,1)S(1)} %get-tuple-element.45), channel_id=1, source_target_pairs={{0,1},{2,3},{1,0},{3,2},{4,5},{6,7},{5,4},{7,6},{8,9},{10,11},{9,8... | collective-permute-start | bytes 196616 | tf_op jit(solution)/shard_map/ppermute | solution.py:558
  19.5 6.8 %copy-start = (bf16[4,2048]{1,0:T(4,128)(2,1)S(1)}, bf16[4,2048]{1,0:T(4,128)(2,1)}, u32[]{:S(2)}) copy-start(bf16[4,2048]{1,0:T(4,128)(2,1)} %param.11) | copy-start | bytes 49156
  19.5 6.8 %copy-start.1 = (s32[2048,1]{0,1:T(1,128)S(1)}, s32[2048,1]{0,1:T(1,128)}, u32[]{:S(2)}) copy-start(s32[2048,1]{0,1:T(1,128)} %param.12) | copy-start | bytes 24580
  19.5 6.8 %copy-start.2 = (s32[2048]{0:T(1024)S(1)}, s32[2048]{0:T(1024)}, u32[]{:S(2)}) copy-start(s32[2048]{0:T(1024)} %param.13) | copy-start | bytes 24580
  22.6 6.3 %collective-permute-start.6 = (f32[8,128]{1,0:T(8,128)S(1)}, f32[8,128]{1,0:T(8,128)S(1)}, u32[]{:S(2)}, u32[]{:S(2)}) collective-permute-start(f32[8,128]{1,0:T(8,128)S(1)} %get-tuple-element.47.by_even_ref), channel_id=1, source_target_pairs={{0,4},{8,12},{16,20},{24,28},{4,0},{12,8},{20,16},{28,24},{1,5},{9... | collective-permute-start | bytes 12296 | tf_op jit(solution)/shard_map/ppermute | solution.py:558
  22.7 6.4 %collective-permute-start.7 = (f32[8,128]{1,0:T(8,128)S(1)}, f32[8,128]{1,0:T(8,128)S(1)}, u32[]{:S(2)}, u32[]{:S(2)}) collective-permute-start(f32[8,128]{1,0:T(8,128)S(1)} %get-tuple-element.48.by_odd_ref), channel_id=1, source_target_pairs={{4,8},{12,16},{20,24},{28,0},{8,4},{16,12},{24,20},{0,28},{5,9},{1... | collective-permute-start | bytes 12296 | tf_op jit(solution)/shard_map/ppermute | solution.py:558
  29.1 3.0 %collective-permute-start.8 = (f32[8,128]{1,0:T(8,128)S(1)}, f32[8,128]{1,0:T(8,128)S(1)}, u32[]{:S(2)}, u32[]{:S(2)}) collective-permute-start(f32[8,128]{1,0:T(8,128)S(1)} %get-tuple-element.56), channel_id=1, source_target_pairs={{1,2},{3,0},{2,1},{0,3},{5,6},{7,4},{6,5},{4,7},{9,10},{11,8},{10,... | collective-permute-start | bytes 12296 | tf_op jit(solution)/shard_map/ppermute | solution.py:558
  29.3 2.9 %collective-permute-start.9 = (f32[8,128]{1,0:T(8,128)S(1)}, f32[8,128]{1,0:T(8,128)S(1)}, u32[]{:S(2)}, u32[]{:S(2)}) collective-permute-start(f32[8,128]{1,0:T(8,128)S(1)} %get-tuple-element.57), channel_id=1, source_target_pairs={{0,1},{2,3},{1,0},{3,2},{4,5},{6,7},{5,4},{7,6},{8,9},{10,11},{9,8... | collective-permute-start | bytes 12296 | tf_op jit(solution)/shard_map/ppermute | solution.py:558

commit v3 on v2

--- a/solution.py
+++ b/solution.py
@@ -19,7 +19,7 @@
 SLAB_X = REACH * BY * BZ
 SLAB_Y = BX * REACH * BZ + 2 * REACH * REACH * BZ
 FIELDS = 4
-STEP = 316
+STEP = 40
 AROUND = [(1, 1), (1, 0), (1, 2), (2, 1), (2, 0), (2, 2), (0, 1), (0, 2)]
 SENDERS = [(1, 0), (1, 1), (1, 2), (2, 0), (2, 1), (2, 2), (0, 1), (0, 2)]
 
@@ -280,7 +280,7 @@
     return {(x, y): value[(x * ny + y) * BZ : (x * ny + y + 1) * BZ] for x in range(nx) for y in range(ny)}
 
 
-def forward_kernel(own, x_even, x_odd, y_even_message, y_odd_message, y_even_ref, y_odd_ref, even_messages_ref, odd_messages_ref):
+def forward_kernel(own, x_even, x_odd, y_even_message, y_odd_message, y_even_ref, y_odd_ref, odd_messages_ref):
     even_y = lax.rem(lax.axis_index("ys"), 2) == 0
     lower, upper = [], []
     for ref, nx in ((own, BX), (x_even, REACH), (x_odd, REACH)):
@@ -290,12 +290,12 @@
     lower, upper = jnp.concatenate(lower, axis=0), jnp.concatenate(upper, axis=0)
     y_even_ref[:SLAB_Y] = jnp.where(even_y, upper, lower).astype(BF)
     y_odd_ref[:SLAB_Y] = jnp.where(even_y, lower, upper).astype(BF)
-    y_even_ref[SLAB_Y:] = y_even_message[...]
+    y_even_ref[SLAB_Y : SLAB_Y + LANES] = y_even_message[...]
     y_odd_ref[SLAB_Y:] = y_odd_message[...]
-    for ref, at in ((even_messages_ref, 0), (odd_messages_ref, 2)):
+    for ref, to, at in ((y_even_ref, SLAB_Y + LANES, 0), (odd_messages_ref, 0, 2)):
         for i, source in enumerate((x_even, x_odd)):
             first = SLAB_X + at * LANES
-            ref[i * LANES : (i + 1) * LANES] = source[first : first + LANES]
+            ref[to + i * LANES : to + (i + 1) * LANES] = source[first : first + LANES]
 
 
 def forward(*operands):
@@ -303,8 +303,8 @@
     return pl.pallas_call(
         forward_kernel,
         in_specs=[vmem] * 5,
-        out_specs=[vmem] * 4,
-        out_shape=[pltpu.VMEM((SLAB_Y + LANES, LANES), BF)] * 2 + [pltpu.VMEM((2 * LANES, LANES), BF)] * 2,
+        out_specs=[vmem] * 3,
+        out_shape=[pltpu.VMEM((rows, LANES), BF) for rows in (SLAB_Y + 3 * LANES, SLAB_Y + LANES, 2 * LANES)],
         compiler_params=pltpu.CompilerParams(vmem_limit_bytes=4 * 2**20),
         name="forward",
     )(*operands)
@@ -359,10 +359,11 @@
     )(own, x_even, x_odd)
 
 
-def messages(x_even, x_odd, y_even, y_odd, even_passed, odd_passed):
+def messages(x_even, x_odd, y_even, y_odd, odd_passed):
     direct = SLAB_X + LANES
     return [
-        (x_even, direct), (even_passed, 0), (odd_passed, 0), (x_odd, direct), (even_passed, LANES), (odd_passed, LANES),
+        (x_even, direct), (y_even, SLAB_Y + LANES), (odd_passed, 0),
+        (x_odd, direct), (y_even, SLAB_Y + 2 * LANES), (odd_passed, LANES),
         (y_even, SLAB_Y), (y_odd, SLAB_Y),
     ]
 
@@ -402,11 +403,11 @@
     )(pinned[0], pinned[1], y_odd, y_even, pinned[2], pinned[3])
 
 
-def answer_kernel(terms, local_ref, x_odd, x_even, y_odd, y_even, odd_passed, even_passed, by_even_ref, by_odd_ref, by_y_ref, tail_ref):
+def answer_kernel(terms, local_ref, x_odd, x_even, y_odd, y_even, odd_passed, by_even_ref, by_odd_ref, by_y_ref, tail_ref):
     local = local_ref[...]
     row = lax.broadcasted_iota(jnp.int32, (8, LANES), 0)
     answers = []
-    for i, (ref, at) in enumerate(messages(x_even, x_odd, y_even, y_odd, even_passed, odd_passed)):
+    for i, (ref, at) in enumerate(messages(x_even, x_odd, y_even, y_odd, odd_passed)):
         x = ref[at : at + LANES, :].astype(F32)
         tail_ref[i : i + 1] = x[terms : terms + 1]
         tail_ref[8 + i : 9 + i] = x[terms + 1 : terms + 2]
@@ -424,7 +425,7 @@
     vmem = pl.BlockSpec(memory_space=pltpu.VMEM)
     return pl.pallas_call(
         functools.partial(answer_kernel, terms),
-        in_specs=[vmem] * 7,
+        in_specs=[vmem] * 6,
         out_specs=[vmem] * 4,
         out_shape=[jax.ShapeDtypeStruct((8, LANES), F32)] * 3 + [jax.ShapeDtypeStruct((16, LANES), F32)],
         compiler_params=pltpu.CompilerParams(vmem_limit_bytes=4 * 2**20),
@@ -575,18 +576,17 @@
     )
     x_even = across("xs", 1, to_x_even)
     x_odd = across("xs", 2, to_x_odd)
-    first = by_operator(translation_ops, 0, 6)
+    first = by_operator(translation_ops, 0, 5)
     x_even, x_odd, first = lax.optimization_barrier((x_even, x_odd, first))
-    to_y_even, to_y_odd, even_messages, odd_messages = forward(own, x_even, x_odd, y_even_message, y_odd_message)
+    to_y_even, to_y_odd, odd_messages = forward(own, x_even, x_odd, y_even_message, y_odd_message)
     y_odd = across("ys", 2, to_y_odd)
     y_even = across("ys", 1, to_y_even)
     odd_messages = across("ys", 2, odd_messages)
-    even_messages = across("ys", 1, even_messages)
-    second = by_operator(translation_ops, 6, 2)
+    second = by_operator(translation_ops, 5, 3)
     inner, along_x = inner_pairs(own, x_even, x_odd)
     local = m2l(inner, along_x, y_odd, y_even, first, second)
     answer_x_even, answer_x_odd, answer_y, tail = answer(
-        num_terms, local, x_odd, x_even, y_odd, y_even, odd_messages, even_messages
+        num_terms, local, x_odd, x_even, y_odd, y_even, odd_messages
     )
 
     back_x_even = across("xs", 1, answer_x_even)

time: 33.3 us -> 33.2 us (level)
  waiting for transfers between devices: 2.2 us -> 1.85 us
    ppermute x10 -> x9, waiting for transfers between devices: 2.2 us -> 1.85 us  [across(): return lax.ppermute(block, axis, pairs + [(b, a) for a, b in pairs])]
    ppermute x10 -> x9, starting transfers between devices: 14.1 us -> 14.1 us  [across(): return lax.ppermute(block, axis, pairs + [(b, a) for a, b in pairs])]
  transfers between devices with their start and end apart: 10 -> 9, of which waited for: 3 -> 4; matrix products, arithmetic and copies ran while one was open for 0% -> 0% of each run, Pallas kernels for 36% -> 36%
where the time goes in v3:
time: 33.2 us; the launch traced here: 32.9 us
  Pallas kernels  16.3 us (49%)
  starting transfers between devices  14.1 us (42%)
  waiting for transfers between devices  1.85 us (6%)
  between operations  0.72 us (2%)
    ppermute x9, starting transfers between devices, across(): return lax.ppermute(block, axis, pairs + [(b, a) for a, b in pairs])  14.1 us
    pallas_call x2, Pallas kernels, by_operator(): pl.pallas_call(functools.partial(by_operator_kernel, first), in_specs=[pl...  6.26 us
    pallas_call x1, Pallas kernels, pack(): pl.pallas_call(functools.partial(pack_kernel, sizes), in_specs=[pl.BlockS...  3.05 us
    pallas_call x1, Pallas kernels, m2l(): pl.pallas_call(m2l_kernel, in_specs=[vmem] * 6, out_specs=vmem, out_shape...  2.88 us
    pallas_call x1, Pallas kernels, atoms_of_device(): pl.pallas_call(functools.partial(atoms_kernel, size_y), in_specs=[whole]...  2.72 us
    ppermute x9, waiting for transfers between devices, across(): return lax.ppermute(block, axis, pairs + [(b, a) for a, b in pairs])  1.85 us
    pallas_call x1, Pallas kernels, merge(): pl.pallas_call(merge_kernel, in_specs=[whole] * 6, out_specs=whole, out_s...  0.96 us
  transfers between devices with their start and end apart: 9, of which 4 were waited for; matrix products, arithmetic and copies ran while one was open for 0% of the time, Pallas kernels for 36%

profile of v3, /device:TPU:0, one launch (start us, length us, event | category | flops | bytes accessed | tf_op | source)
XLA Modules:
  0.0 32.9 jit_solution(16374627899580739394)
XLA Ops:
  0.6 3.1 %pack.1 = (bf16[128,128]{1,0:T(8,128)(2,1)S(1)}, bf16[480,128]{1,0:T(8,128)(2,1)S(1)}, bf16[480,128]{1,0:T(8,128)(2,1)S(1)}, bf16[128,128]{1,0:T(8,128)(2,1)S(1)...) custom-call(s32[16,128]{1,0:T(8,128)} %bitcast.17, ...), custom_call_target="tpu_custom_call" | custom-call | tf_op jit(solution)/shard_map/pack/pallas_call | solution.py:255
  3.7 3.0 %collective-permute-start = (bf16[480,128]{1,0:T(8,128)(2,1)S(1)}, bf16[480,128]{1,0:T(8,128)(2,1)S(1)}, u32[]{:S(2)}, u32[]{:S(2)}) collective-permute-start(bf16[480,128]{1,0:T(8,128)(2,1)S(1)} %get-tuple-element.32), channel_id=1, source_target_pairs={{0,4},{8,12},{16,20},{24,28},{4,0},{12,8},{20,16},{28,24},{1,5},{9... | collective-permute-start | bytes 368648 | tf_op jit(solution)/shard_map/ppermute | solution.py:559
  6.7 3.5 %collective-permute-start.1 = (bf16[480,128]{1,0:T(8,128)(2,1)S(1)}, bf16[480,128]{1,0:T(8,128)(2,1)S(1)}, u32[]{:S(2)}, u32[]{:S(2)}) collective-permute-start(bf16[480,128]{1,0:T(8,128)(2,1)S(1)} %get-tuple-element.33), channel_id=1, source_target_pairs={{4,8},{12,16},{20,24},{28,0},{8,4},{16,12},{24,20},{0,28},{5,9},{1... | collective-permute-start | bytes 368648 | tf_op jit(solution)/shard_map/ppermute | solution.py:559
  10.3 3.6 %by_operator.2.first_ref = bf16[320,80,128]{2,1,0:T(8,128)(2,1)S(1)} custom-call(bf16[121,316,121]{2,1,0:T(8,128)(2,1)} %bitcast.21), custom_call_target="tpu_custom_call" | custom-call | bytes 13107200 | tf_op jit(solution)/shard_map/by_operator/pallas_call | solution.py:73
  13.9 0.0 collective-permute-done.x_even
  13.9 0.4 %collective-permute-done.1.x_odd = bf16[480,128]{1,0:T(8,128)(2,1)S(1)} collective-permute-done((bf16[480,128]{1,0:T(8,128)(2,1)S(1)}, bf16[480,128]{1,0:T(8,128)(2,1)S(1)}, u32[]{:S(2)}, u32[]{:S(2)}) %collective-permute-start.1) | collective-permute-done | bytes 122912 | tf_op jit(solution)/shard_map/ppermute | solution.py:559
  14.3 0.1 collective-permute-start.3
  14.4 1.6 %collective-permute-start.2 = (bf16[368,128]{1,0:T(8,128)(2,1)S(1)}, bf16[368,128]{1,0:T(8,128)(2,1)S(1)}, u32[]{:S(2)}, u32[]{:S(2)}) collective-permute-start(bf16[368,128]{1,0:T(8,128)(2,1)S(1)} %get-tuple-element.40), channel_id=1, source_target_pairs={{1,2},{3,0},{2,1},{0,3},{5,6},{7,4},{6,5},{4,7},{9,10},{11,8},{10,... | collective-permute-start | bytes 282632 | tf_op jit(solution)/shard_map/ppermute | solution.py:559
  16.0 0.2 collective-permute-start.4
  16.2 2.6 %by_operator.3.second_ref = bf16[320,48,128]{2,1,0:T(8,128)(2,1)S(1)} custom-call(bf16[121,316,121]{2,1,0:T(8,128)(2,1)} %bitcast.22), custom_call_target="tpu_custom_call" | custom-call | bytes 7864320 | tf_op jit(solution)/shard_map/by_operator/pallas_call | solution.py:73
  18.9 0.1 inner_pairs.1
  19.0 0.1 collective-permute-done.2.y_odd
  19.1 0.0 collective-permute-done.3.y_even
  19.1 0.0 copy-start
  19.1 0.0 copy-start.1
  19.1 0.0 copy-start.2
  19.1 2.9 %m2l.1.local_ref = bf16[128,128]{1,0:T(8,128)(2,1)S(1)} custom-call(bf16[350,16,128]{2,1,0:T(8,128)(2,1)S(1)} %get-tuple-element.36.inner, f32[10,7,8,128]{3,2,1,0:T(8,128)S(1)} %get-tuple-element.37.along_x, bf16[368,128]{1,0:T(8,128)(2,1)S(1)} %collective-permute-done.2.y_odd, bf16[624,128]{1,0:T(8,128)(2,1)S(1)} %collective-permute-done.3.y_even, ...), custom_call_target="tpu_custom_call" | custom-call | bytes 65536 | tf_op jit(solution)/shard_map/m2l/pallas_call | solution.py:391
  22.0 0.0 collective-permute-done.4.odd_passed
  22.0 0.2 answer.1
  22.2 0.2 collective-permute-start.5
  22.4 3.5 %collective-permute-start.6 = (f32[8,128]{1,0:T(8,128)S(1)}, f32[8,128]{1,0:T(8,128)S(1)}, u32[]{:S(2)}, u32[]{:S(2)}) collective-permute-start(f32[8,128]{1,0:T(8,128)S(1)} %get-tuple-element.46.by_odd_ref), channel_id=1, source_target_pairs={{4,8},{12,16},{20,24},{28,0},{8,4},{16,12},{24,20},{0,28},{5,9},{1... | collective-permute-start | bytes 12296 | tf_op jit(solution)/shard_map/ppermute | solution.py:559
  26.0 0.0 copy-done
  26.0 0.0 copy-done.1
  26.0 0.0 copy-done.2
  26.0 2.7 %atoms.1 = (bf16[121,128]{1,0:T(8,128)(2,1)}, f32[4,2048]{1,0:T(4,128)S(1)}, f32[9,128]{1,0:T(8,128)}) custom-call(s32[16,128]{1,0:T(8,128)S(1)} %bitcast.18, s32[16,128]{1,0:T(8,128)S(1)} %bitcast.20, bf16[64,128]{1,0:T(8,128)(2,1)S(1)} %bitcast.16, bf16[4,128,2048]{2,1,0:T(8,128)(2,1)S(1)} %get-tuple-element.30.rows_ref, ...), custom_call_target="tpu_custom_call" | custom-call | flops 4000000 | bytes 8388608 | tf_op jit(solution)/shard_map/atoms/pallas_call | solution.py:484
  28.7 0.0 collective-permute-done.5.x_even
  28.7 0.1 collective-permute-done.6.x_odd
  28.8 1.9 %collective-permute-start.7 = (f32[8,128]{1,0:T(8,128)S(1)}, f32[8,128]{1,0:T(8,128)S(1)}, u32[]{:S(2)}, u32[]{:S(2)}) collective-permute-start(f32[8,128]{1,0:T(8,128)S(1)} %get-tuple-element.54), channel_id=1, source_target_pairs={{1,2},{3,0},{2,1},{0,3},{5,6},{7,4},{6,5},{4,7},{9,10},{11,8},{10,... | collective-permute-start | bytes 12296 | tf_op jit(solution)/shard_map/ppermute | solution.py:559
  30.6 0.0 collective-permute-start.8
  30.7 1.3 %collective-permute-done.7.y_odd = f32[8,128]{1,0:T(8,128)S(1)} collective-permute-done((f32[8,128]{1,0:T(8,128)S(1)}, f32[8,128]{1,0:T(8,128)S(1)}, u32[]{:S(2)}, u32[]{:S(2)}) %collective-permute-start.7) | collective-permute-done | bytes 4128 | tf_op jit(solution)/shard_map/ppermute | solution.py:559
  32.0 0.0 collective-permute-done.8.y_even
  32.0 1.0 %merge.1 = f32[4,2048]{1,0:T(4,128)} custom-call(f32[4,2048]{1,0:T(4,128)S(1)} %get-tuple-element.50.far_ref, bf16[256,2048]{1,0:T(8,128)(2,1)S(1)} %get-tuple-element.51.place_ref, f32[8,128]{1,0:T(8,128)S(1)} %collective-permute-done.6.x_odd, f32[8,128]{1,0:T(8,128)S(1)} %collective-permute-done.5.x_even, f32[8,128]{1,0:T(8,128)S(1)} %collective-permute-done.7.y_odd, ...), custom_call_target="tpu_custom_call" | custom-call | tf_op jit(solution)/shard_map/merge/pallas_call | solution.py:546
  (2 shorter events, 0.0 us)
Async XLA Ops:
  3.7 10.2 %collective-permute-start = (bf16[480,128]{1,0:T(8,128)(2,1)S(1)}, bf16[480,128]{1,0:T(8,128)(2,1)S(1)}, u32[]{:S(2)}, u32[]{:S(2)}) collective-permute-start(bf16[480,128]{1,0:T(8,128)(2,1)S(1)} %get-tuple-element.32), channel_id=1, source_target_pairs={{0,4},{8,12},{16,20},{24,28},{4,0},{12,8},{20,16},{28,24},{1,5},{9... | collective-permute-start | bytes 368648 | tf_op jit(solution)/shard_map/ppermute | solution.py:559
  6.7 7.6 %collective-permute-start.1 = (bf16[480,128]{1,0:T(8,128)(2,1)S(1)}, bf16[480,128]{1,0:T(8,128)(2,1)S(1)}, u32[]{:S(2)}, u32[]{:S(2)}) collective-permute-start(bf16[480,128]{1,0:T(8,128)(2,1)S(1)} %get-tuple-element.33), channel_id=1, source_target_pairs={{4,8},{12,16},{20,24},{28,0},{8,4},{16,12},{24,20},{0,28},{5,9},{1... | collective-permute-start | bytes 368648 | tf_op jit(solution)/shard_map/ppermute | solution.py:559
  14.3 4.7 %collective-permute-start.3 = (bf16[624,128]{1,0:T(8,128)(2,1)S(1)}, bf16[624,128]{1,0:T(8,128)(2,1)S(1)}, u32[]{:S(2)}, u32[]{:S(2)}) collective-permute-start(bf16[624,128]{1,0:T(8,128)(2,1)S(1)} %get-tuple-element.41), channel_id=1, source_target_pairs={{0,1},{2,3},{1,0},{3,2},{4,5},{6,7},{5,4},{7,6},{8,9},{10,11},{9,8... | collective-permute-start | bytes 479240 | tf_op jit(solution)/shard_map/ppermute | solution.py:559
  14.4 4.7 %collective-permute-start.2 = (bf16[368,128]{1,0:T(8,128)(2,1)S(1)}, bf16[368,128]{1,0:T(8,128)(2,1)S(1)}, u32[]{:S(2)}, u32[]{:S(2)}) collective-permute-start(bf16[368,128]{1,0:T(8,128)(2,1)S(1)} %get-tuple-element.40), channel_id=1, source_target_pairs={{1,2},{3,0},{2,1},{0,3},{5,6},{7,4},{6,5},{4,7},{9,10},{11,8},{10,... | collective-permute-start | bytes 282632 | tf_op jit(solution)/shard_map/ppermute | solution.py:559
  16.0 5.9 %collective-permute-start.4 = (bf16[256,128]{1,0:T(8,128)(2,1)S(1)}, bf16[256,128]{1,0:T(8,128)(2,1)S(1)}, u32[]{:S(2)}, u32[]{:S(2)}) collective-permute-start(bf16[256,128]{1,0:T(8,128)(2,1)S(1)} %get-tuple-element.43), channel_id=1, source_target_pairs={{1,2},{3,0},{2,1},{0,3},{5,6},{7,4},{6,5},{4,7},{9,10},{11,8},{10,... | collective-permute-start | bytes 196616 | tf_op jit(solution)/shard_map/ppermute | solution.py:559
  19.1 6.9 %copy-start = (bf16[4,2048]{1,0:T(4,128)(2,1)S(1)}, bf16[4,2048]{1,0:T(4,128)(2,1)}, u32[]{:S(2)}) copy-start(bf16[4,2048]{1,0:T(4,128)(2,1)} %param.11) | copy-start | bytes 49156
  19.1 6.9 %copy-start.1 = (s32[2048,1]{0,1:T(1,128)S(1)}, s32[2048,1]{0,1:T(1,128)}, u32[]{:S(2)}) copy-start(s32[2048,1]{0,1:T(1,128)} %param.12) | copy-start | bytes 24580
  19.1 6.9 %copy-start.2 = (s32[2048]{0:T(1024)S(1)}, s32[2048]{0:T(1024)}, u32[]{:S(2)}) copy-start(s32[2048]{0:T(1024)} %param.13) | copy-start | bytes 24580
  22.2 6.5 %collective-permute-start.5 = (f32[8,128]{1,0:T(8,128)S(1)}, f32[8,128]{1,0:T(8,128)S(1)}, u32[]{:S(2)}, u32[]{:S(2)}) collective-permute-start(f32[8,128]{1,0:T(8,128)S(1)} %get-tuple-element.45.by_even_ref), channel_id=1, source_target_pairs={{0,4},{8,12},{16,20},{24,28},{4,0},{12,8},{20,16},{28,24},{1,5},{9... | collective-permute-start | bytes 12296 | tf_op jit(solution)/shard_map/ppermute | solution.py:559
  22.4 6.3 %collective-permute-start.6 = (f32[8,128]{1,0:T(8,128)S(1)}, f32[8,128]{1,0:T(8,128)S(1)}, u32[]{:S(2)}, u32[]{:S(2)}) collective-permute-start(f32[8,128]{1,0:T(8,128)S(1)} %get-tuple-element.46.by_odd_ref), channel_id=1, source_target_pairs={{4,8},{12,16},{20,24},{28,0},{8,4},{16,12},{24,20},{0,28},{5,9},{1... | collective-permute-start | bytes 12296 | tf_op jit(solution)/shard_map/ppermute | solution.py:559
  28.8 3.2 %collective-permute-start.7 = (f32[8,128]{1,0:T(8,128)S(1)}, f32[8,128]{1,0:T(8,128)S(1)}, u32[]{:S(2)}, u32[]{:S(2)}) collective-permute-start(f32[8,128]{1,0:T(8,128)S(1)} %get-tuple-element.54), channel_id=1, source_target_pairs={{1,2},{3,0},{2,1},{0,3},{5,6},{7,4},{6,5},{4,7},{9,10},{11,8},{10,... | collective-permute-start | bytes 12296 | tf_op jit(solution)/shard_map/ppermute | solution.py:559
  30.6 1.3 %collective-permute-start.8 = (f32[8,128]{1,0:T(8,128)S(1)}, f32[8,128]{1,0:T(8,128)S(1)}, u32[]{:S(2)}, u32[]{:S(2)}) collective-permute-start(f32[8,128]{1,0:T(8,128)S(1)} %get-tuple-element.55), channel_id=1, source_target_pairs={{0,1},{2,3},{1,0},{3,2},{4,5},{6,7},{5,4},{7,6},{8,9},{10,11},{9,8... | collective-permute-start | bytes 12296 | tf_op jit(solution)/shard_map/ppermute | solution.py:559

commit v4 on v3

--- a/solution.py
+++ b/solution.py
@@ -576,13 +576,13 @@
     )
     x_even = across("xs", 1, to_x_even)
     x_odd = across("xs", 2, to_x_odd)
-    first = by_operator(translation_ops, 0, 5)
+    first = by_operator(translation_ops, 0, 6)
     x_even, x_odd, first = lax.optimization_barrier((x_even, x_odd, first))
     to_y_even, to_y_odd, odd_messages = forward(own, x_even, x_odd, y_even_message, y_odd_message)
     y_odd = across("ys", 2, to_y_odd)
     y_even = across("ys", 1, to_y_even)
     odd_messages = across("ys", 2, odd_messages)
-    second = by_operator(translation_ops, 5, 3)
+    second = by_operator(translation_ops, 6, 2)
     inner, along_x = inner_pairs(own, x_even, x_odd)
     local = m2l(inner, along_x, y_odd, y_even, first, second)
     answer_x_even, answer_x_odd, answer_y, tail = answer(

time: 33.2 us -> 33.2 us (level)
    ppermute x9, waiting for transfers between devices: 1.85 us -> 2.18 us  [across(): return lax.ppermute(block, axis, pairs + [(b, a) for a, b in pairs])]
  transfers between devices with their start and end apart: 9 -> 9, of which waited for: 4 -> 3; matrix products, arithmetic and copies ran while one was open for 0% -> 0% of each run, Pallas kernels for 36% -> 36%
where the time goes in v4:
time: 33.2 us; the launch traced here: 32.9 us
  Pallas kernels  16.1 us (48%)
  starting transfers between devices  13.9 us (42%)
  waiting for transfers between devices  2.18 us (7%)
  between operations  0.73 us (2%)
    ppermute x9, starting transfers between devices, across(): return lax.ppermute(block, axis, pairs + [(b, a) for a, b in pairs])  13.9 us
    pallas_call x2, Pallas kernels, by_operator(): pl.pallas_call(functools.partial(by_operator_kernel, first), in_specs=[pl...  6.06 us
    pallas_call x1, Pallas kernels, pack(): pl.pallas_call(functools.partial(pack_kernel, sizes), in_specs=[pl.BlockS...  3.05 us
    pallas_call x1, Pallas kernels, m2l(): pl.pallas_call(m2l_kernel, in_specs=[vmem] * 6, out_specs=vmem, out_shape...  2.88 us
    pallas_call x1, Pallas kernels, atoms_of_device(): pl.pallas_call(functools.partial(atoms_kernel, size_y), in_specs=[whole]...  2.72 us
    ppermute x9, waiting for transfers between devices, across(): return lax.ppermute(block, axis, pairs + [(b, a) for a, b in pairs])  2.18 us
    pallas_call x1, Pallas kernels, merge(): pl.pallas_call(merge_kernel, in_specs=[whole] * 6, out_specs=whole, out_s...  0.96 us
  transfers between devices with their start and end apart: 9, of which 3 were waited for; matrix products, arithmetic and copies ran while one was open for 0% of the time, Pallas kernels for 36%

profile of v4, /device:TPU:0, one launch (start us, length us, event | category | flops | bytes accessed | tf_op | source)
XLA Modules:
  0.0 32.9 jit_solution(17131890811213107873)
XLA Ops:
  0.6 3.1 %pack.1 = (bf16[128,128]{1,0:T(8,128)(2,1)S(1)}, bf16[480,128]{1,0:T(8,128)(2,1)S(1)}, bf16[480,128]{1,0:T(8,128)(2,1)S(1)}, bf16[128,128]{1,0:T(8,128)(2,1)S(1)...) custom-call(s32[16,128]{1,0:T(8,128)} %bitcast.17, ...), custom_call_target="tpu_custom_call" | custom-call | tf_op jit(solution)/shard_map/pack/pallas_call | solution.py:255
  3.7 3.0 %collective-permute-start = (bf16[480,128]{1,0:T(8,128)(2,1)S(1)}, bf16[480,128]{1,0:T(8,128)(2,1)S(1)}, u32[]{:S(2)}, u32[]{:S(2)}) collective-permute-start(bf16[480,128]{1,0:T(8,128)(2,1)S(1)} %get-tuple-element.32), channel_id=1, source_target_pairs={{0,4},{8,12},{16,20},{24,28},{4,0},{12,8},{20,16},{28,24},{1,5},{9... | collective-permute-start | bytes 368648 | tf_op jit(solution)/shard_map/ppermute | solution.py:559
  6.7 3.5 %collective-permute-start.1 = (bf16[480,128]{1,0:T(8,128)(2,1)S(1)}, bf16[480,128]{1,0:T(8,128)(2,1)S(1)}, u32[]{:S(2)}, u32[]{:S(2)}) collective-permute-start(bf16[480,128]{1,0:T(8,128)(2,1)S(1)} %get-tuple-element.33), channel_id=1, source_target_pairs={{4,8},{12,16},{20,24},{28,0},{8,4},{16,12},{24,20},{0,28},{5,9},{1... | collective-permute-start | bytes 368648 | tf_op jit(solution)/shard_map/ppermute | solution.py:559
  10.3 4.1 %by_operator.2.first_ref = bf16[320,96,128]{2,1,0:T(8,128)(2,1)S(1)} custom-call(bf16[121,316,121]{2,1,0:T(8,128)(2,1)} %bitcast.21), custom_call_target="tpu_custom_call" | custom-call | bytes 15728640 | tf_op jit(solution)/shard_map/by_operator/pallas_call | solution.py:73
  14.4 0.0 collective-permute-done.x_even
  14.4 0.0 collective-permute-done.1.x_odd
  14.4 0.1 collective-permute-start.3
  14.5 1.6 %collective-permute-start.2 = (bf16[368,128]{1,0:T(8,128)(2,1)S(1)}, bf16[368,128]{1,0:T(8,128)(2,1)S(1)}, u32[]{:S(2)}, u32[]{:S(2)}) collective-permute-start(bf16[368,128]{1,0:T(8,128)(2,1)S(1)} %get-tuple-element.40), channel_id=1, source_target_pairs={{1,2},{3,0},{2,1},{0,3},{5,6},{7,4},{6,5},{4,7},{9,10},{11,8},{10,... | collective-permute-start | bytes 282632 | tf_op jit(solution)/shard_map/ppermute | solution.py:559
  16.1 0.2 collective-permute-start.4
  16.3 1.9 %by_operator.3.second_ref = bf16[320,32,128]{2,1,0:T(8,128)(2,1)S(1)} custom-call(bf16[121,316,121]{2,1,0:T(8,128)(2,1)} %bitcast.22), custom_call_target="tpu_custom_call" | custom-call | bytes 5242880 | tf_op jit(solution)/shard_map/by_operator/pallas_call | solution.py:73
  18.3 0.1 inner_pairs.1
  18.4 0.8 %collective-permute-done.2.y_odd = bf16[368,128]{1,0:T(8,128)(2,1)S(1)} collective-permute-done((bf16[368,128]{1,0:T(8,128)(2,1)S(1)}, bf16[368,128]{1,0:T(8,128)(2,1)S(1)}, u32[]{:S(2)}, u32[]{:S(2)}) %collective-permute-start.2) | collective-permute-done | bytes 94240 | tf_op jit(solution)/shard_map/ppermute | solution.py:559
  19.2 0.0 collective-permute-done.3.y_even
  19.2 0.0 copy-start
  19.2 0.0 copy-start.1
  19.2 0.0 copy-start.2
  19.2 2.9 %m2l.1.local_ref = bf16[128,128]{1,0:T(8,128)(2,1)S(1)} custom-call(bf16[350,16,128]{2,1,0:T(8,128)(2,1)S(1)} %get-tuple-element.36.inner, f32[10,7,8,128]{3,2,1,0:T(8,128)S(1)} %get-tuple-element.37.along_x, bf16[368,128]{1,0:T(8,128)(2,1)S(1)} %collective-permute-done.2.y_odd, bf16[624,128]{1,0:T(8,128)(2,1)S(1)} %collective-permute-done.3.y_even, ...), custom_call_target="tpu_custom_call" | custom-call | bytes 65536 | tf_op jit(solution)/shard_map/m2l/pallas_call | solution.py:391
  22.1 0.0 collective-permute-done.4.odd_passed
  22.1 0.2 answer.1
  22.3 0.1 collective-permute-start.5
  22.4 3.5 %collective-permute-start.6 = (f32[8,128]{1,0:T(8,128)S(1)}, f32[8,128]{1,0:T(8,128)S(1)}, u32[]{:S(2)}, u32[]{:S(2)}) collective-permute-start(f32[8,128]{1,0:T(8,128)S(1)} %get-tuple-element.46.by_odd_ref), channel_id=1, source_target_pairs={{4,8},{12,16},{20,24},{28,0},{8,4},{16,12},{24,20},{0,28},{5,9},{1... | collective-permute-start | bytes 12296 | tf_op jit(solution)/shard_map/ppermute | solution.py:559
  26.0 0.0 copy-done
  26.0 0.0 copy-done.1
  26.0 0.0 copy-done.2
  26.0 2.7 %atoms.1 = (bf16[121,128]{1,0:T(8,128)(2,1)}, f32[4,2048]{1,0:T(4,128)S(1)}, f32[9,128]{1,0:T(8,128)}) custom-call(s32[16,128]{1,0:T(8,128)S(1)} %bitcast.18, s32[16,128]{1,0:T(8,128)S(1)} %bitcast.20, bf16[64,128]{1,0:T(8,128)(2,1)S(1)} %bitcast.16, bf16[4,128,2048]{2,1,0:T(8,128)(2,1)S(1)} %get-tuple-element.30.rows_ref, ...), custom_call_target="tpu_custom_call" | custom-call | flops 4000000 | bytes 8388608 | tf_op jit(solution)/shard_map/atoms/pallas_call | solution.py:484
  28.7 0.0 collective-permute-done.5.x_even
  28.7 0.1 collective-permute-done.6.x_odd
  28.8 1.9 %collective-permute-start.7 = (f32[8,128]{1,0:T(8,128)S(1)}, f32[8,128]{1,0:T(8,128)S(1)}, u32[]{:S(2)}, u32[]{:S(2)}) collective-permute-start(f32[8,128]{1,0:T(8,128)S(1)} %get-tuple-element.54), channel_id=1, source_target_pairs={{1,2},{3,0},{2,1},{0,3},{5,6},{7,4},{6,5},{4,7},{9,10},{11,8},{10,... | collective-permute-start | bytes 12296 | tf_op jit(solution)/shard_map/ppermute | solution.py:559
  30.6 0.0 collective-permute-start.8
  30.7 1.3 %collective-permute-done.7.y_odd = f32[8,128]{1,0:T(8,128)S(1)} collective-permute-done((f32[8,128]{1,0:T(8,128)S(1)}, f32[8,128]{1,0:T(8,128)S(1)}, u32[]{:S(2)}, u32[]{:S(2)}) %collective-permute-start.7) | collective-permute-done | bytes 4128 | tf_op jit(solution)/shard_map/ppermute | solution.py:559
  32.0 0.0 collective-permute-done.8.y_even
  32.0 1.0 %merge.1 = f32[4,2048]{1,0:T(4,128)} custom-call(f32[4,2048]{1,0:T(4,128)S(1)} %get-tuple-element.50.far_ref, bf16[256,2048]{1,0:T(8,128)(2,1)S(1)} %get-tuple-element.51.place_ref, f32[8,128]{1,0:T(8,128)S(1)} %collective-permute-done.6.x_odd, f32[8,128]{1,0:T(8,128)S(1)} %collective-permute-done.5.x_even, f32[8,128]{1,0:T(8,128)S(1)} %collective-permute-done.7.y_odd, ...), custom_call_target="tpu_custom_call" | custom-call | tf_op jit(solution)/shard_map/merge/pallas_call | solution.py:546
  (2 shorter events, 0.0 us)
Async XLA Ops:
  3.7 10.7 %collective-permute-start = (bf16[480,128]{1,0:T(8,128)(2,1)S(1)}, bf16[480,128]{1,0:T(8,128)(2,1)S(1)}, u32[]{:S(2)}, u32[]{:S(2)}) collective-permute-start(bf16[480,128]{1,0:T(8,128)(2,1)S(1)} %get-tuple-element.32), channel_id=1, source_target_pairs={{0,4},{8,12},{16,20},{24,28},{4,0},{12,8},{20,16},{28,24},{1,5},{9... | collective-permute-start | bytes 368648 | tf_op jit(solution)/shard_map/ppermute | solution.py:559
  6.7 7.7 %collective-permute-start.1 = (bf16[480,128]{1,0:T(8,128)(2,1)S(1)}, bf16[480,128]{1,0:T(8,128)(2,1)S(1)}, u32[]{:S(2)}, u32[]{:S(2)}) collective-permute-start(bf16[480,128]{1,0:T(8,128)(2,1)S(1)} %get-tuple-element.33), channel_id=1, source_target_pairs={{4,8},{12,16},{20,24},{28,0},{8,4},{16,12},{24,20},{0,28},{5,9},{1... | collective-permute-start | bytes 368648 | tf_op jit(solution)/shard_map/ppermute | solution.py:559
  14.4 4.7 %collective-permute-start.3 = (bf16[624,128]{1,0:T(8,128)(2,1)S(1)}, bf16[624,128]{1,0:T(8,128)(2,1)S(1)}, u32[]{:S(2)}, u32[]{:S(2)}) collective-permute-start(bf16[624,128]{1,0:T(8,128)(2,1)S(1)} %get-tuple-element.41), channel_id=1, source_target_pairs={{0,1},{2,3},{1,0},{3,2},{4,5},{6,7},{5,4},{7,6},{8,9},{10,11},{9,8... | collective-permute-start | bytes 479240 | tf_op jit(solution)/shard_map/ppermute | solution.py:559
  14.5 4.6 %collective-permute-start.2 = (bf16[368,128]{1,0:T(8,128)(2,1)S(1)}, bf16[368,128]{1,0:T(8,128)(2,1)S(1)}, u32[]{:S(2)}, u32[]{:S(2)}) collective-permute-start(bf16[368,128]{1,0:T(8,128)(2,1)S(1)} %get-tuple-element.40), channel_id=1, source_target_pairs={{1,2},{3,0},{2,1},{0,3},{5,6},{7,4},{6,5},{4,7},{9,10},{11,8},{10,... | collective-permute-start | bytes 282632 | tf_op jit(solution)/shard_map/ppermute | solution.py:559
  16.1 5.9 %collective-permute-start.4 = (bf16[256,128]{1,0:T(8,128)(2,1)S(1)}, bf16[256,128]{1,0:T(8,128)(2,1)S(1)}, u32[]{:S(2)}, u32[]{:S(2)}) collective-permute-start(bf16[256,128]{1,0:T(8,128)(2,1)S(1)} %get-tuple-element.43), channel_id=1, source_target_pairs={{1,2},{3,0},{2,1},{0,3},{5,6},{7,4},{6,5},{4,7},{9,10},{11,8},{10,... | collective-permute-start | bytes 196616 | tf_op jit(solution)/shard_map/ppermute | solution.py:559
  19.2 6.8 %copy-start = (bf16[4,2048]{1,0:T(4,128)(2,1)S(1)}, bf16[4,2048]{1,0:T(4,128)(2,1)}, u32[]{:S(2)}) copy-start(bf16[4,2048]{1,0:T(4,128)(2,1)} %param.11) | copy-start | bytes 49156
  19.2 6.8 %copy-start.1 = (s32[2048,1]{0,1:T(1,128)S(1)}, s32[2048,1]{0,1:T(1,128)}, u32[]{:S(2)}) copy-start(s32[2048,1]{0,1:T(1,128)} %param.12) | copy-start | bytes 24580
  19.2 6.8 %copy-start.2 = (s32[2048]{0:T(1024)S(1)}, s32[2048]{0:T(1024)}, u32[]{:S(2)}) copy-start(s32[2048]{0:T(1024)} %param.13) | copy-start | bytes 24580
  22.3 6.4 %collective-permute-start.5 = (f32[8,128]{1,0:T(8,128)S(1)}, f32[8,128]{1,0:T(8,128)S(1)}, u32[]{:S(2)}, u32[]{:S(2)}) collective-permute-start(f32[8,128]{1,0:T(8,128)S(1)} %get-tuple-element.45.by_even_ref), channel_id=1, source_target_pairs={{0,4},{8,12},{16,20},{24,28},{4,0},{12,8},{20,16},{28,24},{1,5},{9... | collective-permute-start | bytes 12296 | tf_op jit(solution)/shard_map/ppermute | solution.py:559
  22.4 6.4 %collective-permute-start.6 = (f32[8,128]{1,0:T(8,128)S(1)}, f32[8,128]{1,0:T(8,128)S(1)}, u32[]{:S(2)}, u32[]{:S(2)}) collective-permute-start(f32[8,128]{1,0:T(8,128)S(1)} %get-tuple-element.46.by_odd_ref), channel_id=1, source_target_pairs={{4,8},{12,16},{20,24},{28,0},{8,4},{16,12},{24,20},{0,28},{5,9},{1... | collective-permute-start | bytes 12296 | tf_op jit(solution)/shard_map/ppermute | solution.py:559
  28.8 3.2 %collective-permute-start.7 = (f32[8,128]{1,0:T(8,128)S(1)}, f32[8,128]{1,0:T(8,128)S(1)}, u32[]{:S(2)}, u32[]{:S(2)}) collective-permute-start(f32[8,128]{1,0:T(8,128)S(1)} %get-tuple-element.54), channel_id=1, source_target_pairs={{1,2},{3,0},{2,1},{0,3},{5,6},{7,4},{6,5},{4,7},{9,10},{11,8},{10,... | collective-permute-start | bytes 12296 | tf_op jit(solution)/shard_map/ppermute | solution.py:559
  30.6 1.3 %collective-permute-start.8 = (f32[8,128]{1,0:T(8,128)S(1)}, f32[8,128]{1,0:T(8,128)S(1)}, u32[]{:S(2)}, u32[]{:S(2)}) collective-permute-start(f32[8,128]{1,0:T(8,128)S(1)} %get-tuple-element.55), channel_id=1, source_target_pairs={{0,1},{2,3},{1,0},{3,2},{4,5},{6,7},{5,4},{7,6},{8,9},{10,11},{9,8... | collective-permute-start | bytes 12296 | tf_op jit(solution)/shard_map/ppermute | solution.py:559
